TPU v7x, 32 devices: a whole 2x2x4 slice. The times are simulated.
32 devices in a mesh: section: 4 (over y, core), dp: 8 (over z, x).
Axes of the slice: x: 2, y: 2, z: 4, core: 2. Of those that a mesh axis runs over, the one named last changes fastest.
Arguments:
- activations: bfloat16 [2, 8, 1152, 512], P(None, 'dp', 'section'), may hold values from -6 to 6
- cotangent: bfloat16 [2, 8, 1152, 512], P(None, 'dp', 'section'), may hold values from -6 to 6
- article_ids: int32 [2, 8, 1152], P(None, 'dp'), may hold values from 0 to 2, as said below
- section_proj: bfloat16 [4, 512, 1536], P('section'), may hold values from -0.25 to 0.25
- out_rows: bfloat16 [1024, 512], P('section'), may hold values from -1.5 to 1.5
- up_rows: bfloat16 [1024, 2048], P('section'), may hold values from -0.25 to 0.25
- down_rows: bfloat16 [4096, 512], P('section'), may hold values from -0.125 to 0.125
- norm_gains: bfloat16 [4, 512], P('section'), may hold values from 0.5 to 1.5
- slopes: bfloat16 [4, 4], P('section'), may hold values from 0.0029907227 to 0.099609375
Outputs:
- results: bfloat16 [2, 8, 1152, 512], P(None, 'dp', 'section')
- input_grad: float32 [2, 8, 1152, 512], P(None, 'dp', 'section')
- grad_section_proj: float32 [4, 512, 1536], P('section')
- grad_out_rows: float32 [1024, 512], P('section')
- grad_up_rows: float32 [1024, 2048], P('section')
- grad_down_rows: float32 [4096, 512], P('section')
- grad_norm_gains: float32 [4, 512], P('section')
- grad_slopes: float32 [4, 4], P('section')
Inputs may be any that keep to these rules, and one draw needn't show every extreme that they name: `article_ids`: along each row the ids never fall and every row holds the three articles 0, 1 and 2; in every row one of them holds bytes of both the first and the last quarter of the row.
All inputs are finite; a program needn't handle non-finite values.
Results may differ from a plain program's by a relative error of at most 0.025.
Values may be sent and summed in bfloat16 or wider, within the bound.
A program may use at most 448 MiB of HBM per device.

v0:
```python
import jax
import jax.numpy as jnp
from jax import lax
from jax.sharding import PartitionSpec as P

EPSILON = 1e-05
MASKED = -1e30


def passed_along(value, axis, steps):
    count = lax.axis_size(axis)
    first, last = (max(0, -steps), min(count, count - steps))
    return lax.ppermute(value, axis, [(source, source + steps) for source in range(first, last)])


def as_sent(shard):

    def short(part):
        return part.astype(jnp.bfloat16) if part.dtype == jnp.float32 else part

    return jax.tree.map(short, shard)


def norm_pieces(value):
    centred = value - jnp.mean(value, axis=-1, keepdims=True)
    inverse_deviation = lax.rsqrt(jnp.mean(centred * centred, axis=-1, keepdims=True) + EPSILON)
    return (centred * inverse_deviation, inverse_deviation)


def norm_backward_pass(normalized_gradient, gain_vector, standardized_rows, inverse_deviation):
    scaled_rows = normalized_gradient * gain_vector
    centred = (
        scaled_rows
        - jnp.mean(scaled_rows, axis=-1, keepdims=True)
        - standardized_rows * jnp.mean(scaled_rows * standardized_rows, axis=-1, keepdims=True)
    )
    gradient_of_gain = jnp.sum(
        normalized_gradient * standardized_rows, axis=tuple(range(normalized_gradient.ndim - 1))
    )
    return (centred * inverse_deviation, gradient_of_gain)


def matmul(left, right):
    return lax.dot_general(
        left, right, (((left.ndim - 1,), (0,)), ((), ())), preferred_element_type=jnp.float32
    )


def product_with_transpose(left, right):
    return lax.dot_general(
        left, right, (((left.ndim - 1,), (1,)), ((), ())), preferred_element_type=jnp.float32
    )


def outer_sum(left, right):
    leading = tuple(range(left.ndim - 1))
    return lax.dot_general(
        left, right, ((leading, leading), ((), ())), preferred_element_type=jnp.float32
    )


def blocks_of(length):
    block_count = max(1, length // 512)
    return (block_count, length // block_count)


def block_scores(
    queries, key_rows, id_rows, slope_heads, row_start, row_stop, head_start, head_stop, score_scale
):
    raw_scores = (
        jnp.einsum(
            "bqhd,bkhd->bhqk",
            queries[:, row_start:row_stop, head_start:head_stop],
            key_rows[:, :row_stop, head_start:head_stop],
            preferred_element_type=jnp.float32,
        )
        * score_scale
    )
    distance = (jnp.arange(row_start, row_stop)[:, None] - jnp.arange(row_stop)[None, :]).astype(
        jnp.float32
    )
    raw_scores = raw_scores - slope_heads[head_start:head_stop][None, :, None, None] * distance
    allowed = (distance >= 0)[None, None] & (
        id_rows[:, row_start:row_stop, None] == id_rows[:, None, :row_stop]
    )[:, None]
    return (jnp.where(allowed, raw_scores, MASKED), distance)


def attend(queries, key_rows, value_rows, id_rows, slope_heads):
    batch_rows, length, head_count, head_dim = queries.shape
    score_scale = head_dim ** (-0.5)
    block_count, block_size = blocks_of(length)
    head_group = max(1, head_count // 2)
    out_blocks = []
    lse_blocks = []
    for block_index in range(block_count):
        row_start = block_index * block_size
        row_stop = row_start + block_size
        head_parts = []
        lse_parts = []
        for head_start in range(0, head_count, head_group):
            head_stop = head_start + head_group
            scores, distance = block_scores(
                queries,
                key_rows,
                id_rows,
                slope_heads,
                row_start,
                row_stop,
                head_start,
                head_stop,
                score_scale,
            )
            highest = jnp.max(scores, axis=-1, keepdims=True)
            exps = jnp.exp(scores - highest)
            denominator = jnp.sum(exps, axis=-1, keepdims=True)
            weights_soft = (exps / denominator).astype(jnp.bfloat16)
            lse_parts.append((highest + jnp.log(denominator))[..., 0])
            head_parts.append(
                jnp.einsum(
                    "bhqk,bkhd->bqhd",
                    weights_soft,
                    value_rows[:, :row_stop, head_start:head_stop],
                    preferred_element_type=jnp.float32,
                )
            )
        out_blocks.append(jnp.concatenate(head_parts, axis=2))
        lse_blocks.append(jnp.concatenate(lse_parts, axis=1))
    return (
        jnp.concatenate(out_blocks, axis=1).astype(jnp.bfloat16),
        jnp.concatenate(lse_blocks, axis=2),
    )


def attend_back(queries, key_rows, value_rows, id_rows, slope_heads, lse_rows, grad_rows):
    batch_rows, length, head_count, head_dim = queries.shape
    score_scale = head_dim ** (-0.5)
    block_count, block_size = blocks_of(length)
    head_group = max(1, head_count // 2)
    grad_keys = jnp.zeros(queries.shape, jnp.float32)
    grad_values = jnp.zeros(queries.shape, jnp.float32)
    slope_grad = jnp.zeros((head_count,), jnp.float32)
    query_blocks = []
    for block_index in range(block_count):
        row_start = block_index * block_size
        row_stop = row_start + block_size
        head_parts = []
        for head_start in range(0, head_count, head_group):
            head_stop = head_start + head_group
            scores, distance = block_scores(
                queries,
                key_rows,
                id_rows,
                slope_heads,
                row_start,
                row_stop,
                head_start,
                head_stop,
                score_scale,
            )
            weights_now = jnp.exp(
                scores - lse_rows[:, head_start:head_stop, row_start:row_stop, None]
            )
            grad_here = grad_rows[:, row_start:row_stop, head_start:head_stop]
            grad_weights = jnp.einsum(
                "bqhd,bkhd->bhqk",
                grad_here,
                value_rows[:, :row_stop, head_start:head_stop],
                preferred_element_type=jnp.float32,
            )
            centre = jnp.sum(weights_now * grad_weights, axis=-1, keepdims=True)
            grad_scores = (weights_now * (grad_weights - centre)).astype(jnp.bfloat16)
            slope_grad = slope_grad.at[head_start:head_stop].add(
                -jnp.sum(grad_scores.astype(jnp.float32) * distance, axis=(0, 2, 3))
            )
            head_parts.append(
                jnp.einsum(
                    "bhqk,bkhd->bqhd",
                    grad_scores,
                    key_rows[:, :row_stop, head_start:head_stop],
                    preferred_element_type=jnp.float32,
                )
                * score_scale
            )
            grad_keys = grad_keys.at[:, :row_stop, head_start:head_stop].add(
                jnp.einsum(
                    "bhqk,bqhd->bkhd",
                    grad_scores,
                    queries[:, row_start:row_stop, head_start:head_stop],
                    preferred_element_type=jnp.float32,
                )
                * score_scale
            )
            grad_values = grad_values.at[:, :row_stop, head_start:head_stop].add(
                jnp.einsum(
                    "bhqk,bqhd->bkhd",
                    weights_now.astype(jnp.bfloat16),
                    grad_here,
                    preferred_element_type=jnp.float32,
                )
            )
        query_blocks.append(jnp.concatenate(head_parts, axis=2))
    return (jnp.concatenate(query_blocks, axis=1), grad_keys, grad_values, slope_grad)


def block_forward(hidden_state, id_rows, weight_group):
    query_key_value_weight, out_weight, expansion_weight, down_weight, paired_gains, slope_heads = (
        weight_group
    )
    batch_rows, length, width = hidden_state.shape
    head_count = slope_heads.shape[0]
    first_standardized, first_inverse_deviation = norm_pieces(hidden_state)
    normalized_rows = (first_standardized * paired_gains[0]).astype(jnp.bfloat16)
    mixed = (
        matmul(normalized_rows, query_key_value_weight)
        .astype(jnp.bfloat16)
        .reshape(batch_rows, length, 3, head_count, width // head_count)
    )
    queries = mixed[:, :, 0]
    key_rows = mixed[:, :, 1]
    value_rows = mixed[:, :, 2]
    attended, lse_rows = attend(queries, key_rows, value_rows, id_rows, slope_heads)
    attended = attended.reshape(batch_rows, length, width)
    middle_state = hidden_state + matmul(attended, out_weight)
    second_standardized, second_inverse_deviation = norm_pieces(middle_state)
    second_normalized = (second_standardized * paired_gains[1]).astype(jnp.bfloat16)
    up_raw = matmul(second_normalized, expansion_weight)
    activ = jax.nn.gelu(up_raw).astype(jnp.bfloat16)
    result = middle_state + matmul(activ, down_weight)
    return (result, (hidden_state, queries, key_rows, value_rows, lse_rows, attended, middle_state))


def block_backward(grad_result, kept, id_rows, weight_group):
    query_key_value_weight, out_weight, expansion_weight, down_weight, paired_gains, slope_heads = (
        weight_group
    )
    hidden_state, queries, key_rows, value_rows, lse_rows, attended, middle_state = kept
    batch_rows, length, width = hidden_state.shape
    grad_branch = grad_result.astype(jnp.bfloat16)
    second_standardized, second_inverse_deviation = norm_pieces(middle_state)
    second_normalized = (second_standardized * paired_gains[1]).astype(jnp.bfloat16)
    up_raw = matmul(second_normalized, expansion_weight)
    activ = jax.nn.gelu(up_raw).astype(jnp.bfloat16)
    grad_down = outer_sum(activ, grad_branch)
    grad_activ = product_with_transpose(grad_branch, down_weight)
    unscaled_up_gradient = jax.vjp(jax.nn.gelu, up_raw)[1](grad_activ)[0].astype(jnp.bfloat16)
    grad_up = outer_sum(second_normalized, unscaled_up_gradient)
    back_two, gain_grad_two = norm_backward_pass(
        product_with_transpose(unscaled_up_gradient, expansion_weight),
        paired_gains[1],
        second_standardized,
        second_inverse_deviation,
    )
    grad_middle = grad_result + back_two
    grad_att_in = grad_middle.astype(jnp.bfloat16)
    grad_out_weight = outer_sum(attended, grad_att_in)
    grad_attended = (
        product_with_transpose(grad_att_in, out_weight).astype(jnp.bfloat16).reshape(queries.shape)
    )
    grad_query, grad_keys, grad_values, slope_grad = attend_back(
        queries, key_rows, value_rows, id_rows, slope_heads, lse_rows, grad_attended
    )
    mixed_gradient = jnp.concatenate(
        [
            grad_query.reshape(batch_rows, length, width),
            grad_keys.reshape(batch_rows, length, width),
            grad_values.reshape(batch_rows, length, width),
        ],
        axis=-1,
    ).astype(jnp.bfloat16)
    first_standardized, first_inverse_deviation = norm_pieces(hidden_state)
    first_normalized = (first_standardized * paired_gains[0]).astype(jnp.bfloat16)
    grad_qkv = outer_sum(first_normalized, mixed_gradient)
    back_one, gain_grad_one = norm_backward_pass(
        product_with_transpose(mixed_gradient, query_key_value_weight),
        paired_gains[0],
        first_standardized,
        first_inverse_deviation,
    )
    grad_hidden = grad_middle + back_one
    return (
        grad_hidden,
        (
            grad_qkv,
            (
                grad_out_weight,
                grad_up,
                grad_down,
                jnp.stack([gain_grad_one, gain_grad_two]),
                slope_grad,
            ),
        ),
    )


def grouped_rows(long_rows, id_rows):
    batch_rows, length, width = long_rows.shape
    earlier = jnp.concatenate([jnp.full((batch_rows, 2), -1, jnp.int32), id_rows[:, :-2]], axis=1)
    keep_rows = earlier == id_rows
    moved = jnp.concatenate(
        [jnp.zeros((batch_rows, 2, width), long_rows.dtype), long_rows[:, :-2]], axis=1
    )
    shifted = jnp.where(keep_rows[..., None], moved, jnp.zeros_like(moved))
    return (shifted.reshape(batch_rows, length // 3, 3 * width), keep_rows)


def pool_forward(long_rows, id_rows, pool_weight):
    grouped, keep_rows = grouped_rows(long_rows, id_rows)
    return product_with_transpose(grouped, pool_weight).astype(jnp.bfloat16)


def pool_backward(long_rows, grad_pooled, id_rows, pool_weight):
    batch_rows, length, width = long_rows.shape
    grouped, keep_rows = grouped_rows(long_rows, id_rows)
    grad_weight = outer_sum(grad_pooled, grouped)
    grad_grouped = matmul(grad_pooled, pool_weight).reshape(batch_rows, length, width)
    masked = jnp.where(keep_rows[..., None], grad_grouped, jnp.zeros_like(grad_grouped))
    grad_long = jnp.concatenate(
        [masked[:, 2:], jnp.zeros((batch_rows, 2, width), jnp.float32)], axis=1
    )
    return (grad_weight, grad_long)


def up_forward(short_rows, skip_rows, expansion_weight):
    batch_rows, short_len, width = short_rows.shape
    raised = matmul(short_rows, expansion_weight).reshape(batch_rows, 3 * short_len, width)
    return (raised + skip_rows.astype(jnp.float32)).astype(jnp.bfloat16)


def up_backward(short_rows, grad_rows, expansion_weight):
    batch_rows, short_len, width = short_rows.shape
    grouped = grad_rows.reshape(batch_rows, short_len, 3 * width)
    grad_weight = outer_sum(short_rows, grouped)
    return (grad_weight, product_with_transpose(grouped, expansion_weight).astype(jnp.bfloat16))


def pick_slot(buffers, slot_index):

    def pick_one(whole_buf):
        return lax.dynamic_index_in_dim(whole_buf, slot_index, 0, keepdims=False)

    return jax.tree.map(pick_one, buffers)


def store_slot(buffers, values, slot_index):

    def store_one(whole_buf, piece_val):
        return lax.dynamic_update_index_in_dim(
            whole_buf, piece_val.astype(whole_buf.dtype), slot_index, 0
        )

    return jax.tree.map(store_one, buffers, values)


def kept_zeros(leading, batch_rows, length, width, head_count):
    head_dim = width // head_count
    return (
        jnp.zeros(leading + (batch_rows, length, width), jnp.float32),
        jnp.zeros(leading + (batch_rows, length, head_count, head_dim), jnp.bfloat16),
        jnp.zeros(leading + (batch_rows, length, head_count, head_dim), jnp.bfloat16),
        jnp.zeros(leading + (batch_rows, length, head_count, head_dim), jnp.bfloat16),
        jnp.zeros(leading + (batch_rows, head_count, length), jnp.float32),
        jnp.zeros(leading + (batch_rows, length, width), jnp.bfloat16),
        jnp.zeros(leading + (batch_rows, length, width), jnp.float32),
    )


def body(
    activations,
    cotangent,
    article_ids,
    section_proj,
    out_rows,
    up_rows,
    down_rows,
    norm_gains,
    slopes,
):
    section_count = lax.axis_size("section")
    section_id = lax.axis_index("section")
    micro = activations.shape[0]
    batch_rows = activations.shape[1]
    width = activations.shape[3]
    hidden_units = up_rows.shape[1]
    head_count = 2 * slopes.shape[1]
    full_acts, full_cot = (
        lax.all_gather(activations, "section", axis=2, tiled=True),
        lax.all_gather(cotangent, "section", axis=2, tiled=True),
    )
    length = full_acts.shape[2]
    short_len = length // 3
    short_ids = article_ids.reshape(micro, batch_rows, short_len, 3)[..., 0]
    partner = passed_along((out_rows, up_rows, down_rows, norm_gains, slopes), "section", -1)
    own_proj = section_proj[0]
    block_weights = (
        own_proj,
        jnp.concatenate([out_rows, partner[0]], axis=0),
        jnp.concatenate([up_rows, partner[1]], axis=0),
        jnp.concatenate([down_rows, partner[2]], axis=0),
        jnp.concatenate([norm_gains, partner[3]], axis=0).astype(jnp.float32),
        jnp.concatenate([slopes, partner[4]], axis=1).reshape(-1).astype(jnp.float32),
    )
    long_zero = jnp.zeros((batch_rows, length, width), jnp.bfloat16)
    short_zero = jnp.zeros((batch_rows, short_len, width), jnp.bfloat16)
    long_kept_zero = kept_zeros((), batch_rows, length, width, head_count)
    short_kept_zero = kept_zeros((), batch_rows, short_len, width, head_count)
    tick_total = micro + section_count - 1
    tick_numbers = jnp.arange(tick_total, dtype=jnp.int32)

    def forward_one(received):
        long_in, short_in, skip_rows, slot_index = received
        hidden_state = pick_slot(full_acts, slot_index).astype(jnp.float32)
        result, kept = block_forward(
            hidden_state, pick_slot(article_ids, slot_index), block_weights
        )
        sent = result.astype(jnp.bfloat16)
        return ((sent, short_zero, sent), (kept, short_kept_zero, long_zero, short_zero, long_zero))

    def forward_two(received):
        long_in, short_in, skip_rows, slot_index = received
        pooled = pool_forward(long_in, pick_slot(article_ids, slot_index), own_proj)
        return (
            (long_zero, pooled, long_zero),
            (long_kept_zero, short_kept_zero, long_in, short_zero, long_zero),
        )

    def forward_three(received):
        long_in, short_in, skip_rows, slot_index = received
        result, kept = block_forward(
            short_in.astype(jnp.float32), pick_slot(short_ids, slot_index), block_weights
        )
        return (
            (long_zero, result.astype(jnp.bfloat16), long_zero),
            (long_kept_zero, kept, long_zero, short_zero, long_zero),
        )

    def forward_four(received):
        long_in, short_in, skip_rows, slot_index = received
        outputs = up_forward(short_in, skip_rows, own_proj)
        return (
            (long_zero, short_zero, long_zero),
            (long_kept_zero, short_kept_zero, long_zero, short_in, outputs),
        )

    def forward_spare(received):
        return (
            (long_zero, short_zero, long_zero),
            (long_kept_zero, short_kept_zero, long_zero, short_zero, long_zero),
        )

    def forward_tick(carry, tick_index):
        state, recv_long, recv_short, skip_buffer = carry
        micro_index = tick_index - section_id
        active = (micro_index >= 0) & (micro_index < micro)
        slot_index = jnp.clip(micro_index, 0, micro - 1)
        write_index = jnp.where(active, slot_index, micro)
        branch_index = jnp.where(active, section_id, section_count)
        skip_rows = pick_slot(skip_buffer, slot_index)
        sends, stores = lax.switch(
            branch_index,
            [forward_one, forward_two, forward_three, forward_four, forward_spare],
            (recv_long, recv_short, skip_rows, slot_index),
        )
        state = store_slot(state, stores, write_index)
        recv_long, recv_short = passed_along((as_sent(sends[0]), as_sent(sends[1])), "section", 1)
        arrived = passed_along(as_sent(sends[2]), "section", section_count - 1)
        store_index = jnp.where(tick_index < micro, tick_index, micro)
        skip_buffer = store_slot(skip_buffer, arrived, store_index)
        return ((state, recv_long, recv_short, skip_buffer), None)

    slots = micro + 1
    state = (
        kept_zeros((slots,), batch_rows, length, width, head_count),
        kept_zeros((slots,), batch_rows, short_len, width, head_count),
        jnp.zeros((slots, batch_rows, length, width), jnp.bfloat16),
        jnp.zeros((slots, batch_rows, short_len, width), jnp.bfloat16),
        jnp.zeros((slots, batch_rows, length, width), jnp.bfloat16),
    )
    skip_buffer = jnp.zeros((slots, batch_rows, length, width), jnp.bfloat16)
    forward_carry, unused_rows = lax.scan(
        forward_tick, (state, long_zero, short_zero, skip_buffer), tick_numbers
    )
    state = forward_carry[0]
    long_kept, short_kept, pool_kept, up_kept, result_buffer = state
    back_zero = jnp.zeros((batch_rows, length, width), jnp.float32)
    input_zero = jnp.zeros((batch_rows, length, width), jnp.float32)

    def add_grads(back_state, proj_grad, block_grads):
        new_block = jax.tree.map(jnp.add, back_state[1], block_grads)
        return (back_state[0] + proj_grad, new_block)

    def backward_four(back_state, received):
        long_in, short_in, skip_grad, slot_index = received
        grad_rows = pick_slot(full_cot, slot_index)
        grad_proj, grad_short = up_backward(pick_slot(up_kept, slot_index), grad_rows, own_proj)
        return (
            (back_state[0] + grad_proj, back_state[1]),
            (back_zero, grad_short, grad_rows),
            input_zero,
        )

    def backward_three(back_state, received):
        long_in, short_in, skip_grad, slot_index = received
        grad_hidden, grads = block_backward(
            short_in.astype(jnp.float32),
            pick_slot(short_kept, slot_index),
            pick_slot(short_ids, slot_index),
            block_weights,
        )
        return (
            add_grads(back_state, grads[0], grads[1]),
            (back_zero, grad_hidden.astype(jnp.bfloat16), long_zero),
            input_zero,
        )

    def backward_two(back_state, received):
        long_in, short_in, skip_grad, slot_index = received
        grad_proj, grad_long = pool_backward(
            pick_slot(pool_kept, slot_index), short_in, pick_slot(article_ids, slot_index), own_proj
        )
        return (
            (back_state[0] + grad_proj, back_state[1]),
            (grad_long, short_zero, long_zero),
            input_zero,
        )

    def backward_one(back_state, received):
        long_in, short_in, skip_grad, slot_index = received
        incoming = (
            (long_in + skip_grad.astype(jnp.float32)).astype(jnp.bfloat16).astype(jnp.float32)
        )
        grad_hidden, grads = block_backward(
            incoming,
            pick_slot(long_kept, slot_index),
            pick_slot(article_ids, slot_index),
            block_weights,
        )
        return (
            add_grads(back_state, grads[0], grads[1]),
            (back_zero, short_zero, long_zero),
            grad_hidden,
        )

    def backward_spare(back_state, received):
        return (back_state, (back_zero, short_zero, long_zero), input_zero)

    def backward_tick(carry, tick_index):
        back_state, input_buffer, recv_long, recv_short, skip_grads = carry
        micro_index = tick_index - (section_count - 1 - section_id)
        active = (micro_index >= 0) & (micro_index < micro)
        slot_index = jnp.clip(micro_index, 0, micro - 1)
        write_index = jnp.where(active, slot_index, micro)
        branch_index = jnp.where(active, section_id, section_count)
        skip_grad = pick_slot(skip_grads, slot_index)
        back_state, sends, input_value = lax.switch(
            branch_index,
            [backward_one, backward_two, backward_three, backward_four, backward_spare],
            back_state,
            (recv_long, recv_short, skip_grad, slot_index),
        )
        input_buffer = store_slot(input_buffer, input_value, write_index)
        recv_long, arrived_short = passed_along(
            (sends[0], sends[1].astype(jnp.float32)), "section", -1
        )
        recv_short = arrived_short.astype(jnp.bfloat16)
        arrived = passed_along(as_sent(sends[2]), "section", -(section_count - 1))
        store_index = jnp.where(tick_index < micro, tick_index, micro)
        skip_grads = store_slot(skip_grads, arrived, store_index)
        return ((back_state, input_buffer, recv_long, recv_short, skip_grads), None)

    back_state = (
        jnp.zeros(own_proj.shape, jnp.float32),
        (
            jnp.zeros((width, width), jnp.float32),
            jnp.zeros((width, hidden_units), jnp.float32),
            jnp.zeros((hidden_units, width), jnp.float32),
            jnp.zeros((2, width), jnp.float32),
            jnp.zeros((head_count,), jnp.float32),
        ),
    )
    input_buffer = jnp.zeros((slots, batch_rows, length, width), jnp.float32)
    skip_grads = jnp.zeros((slots, batch_rows, length, width), jnp.bfloat16)
    backward_carry, unused_grads = lax.scan(
        backward_tick, (back_state, input_buffer, back_zero, short_zero, skip_grads), tick_numbers
    )
    back_state = backward_carry[0]
    input_buffer = backward_carry[1][:micro]
    result_buffer = result_buffer[:micro]
    proj_grad, block_grads = back_state
    half_width = width // 2
    half_units = hidden_units // 2
    half_heads = head_count // 2
    even_section = section_id % 2 == 0

    def lower_halves(grads):
        return (
            grads[0][:half_width],
            grads[1][:half_width],
            grads[2][:half_units],
            grads[3][:1],
            grads[4][:half_heads],
        )

    summed = lax.psum((proj_grad,) + tuple(block_grads), "dp")
    grads = summed[1:]
    handed = passed_along(
        (
            grads[0][half_width:],
            grads[1][half_width:],
            grads[2][half_units:],
            grads[3][1:],
            grads[4][half_heads:],
        ),
        "section",
        1,
    )
    shares = tuple(
        (
            jnp.where(even_section, own_part, other_part)
            for own_part, other_part in zip(lower_halves(summed[1:]), handed)
        )
    )
    proj_total = summed[0]
    results_part, input_part = (
        lax.psum_scatter(
            result_buffer.astype(jnp.float32), "section", scatter_dimension=2, tiled=True
        ),
        lax.psum_scatter(input_buffer, "section", scatter_dimension=2, tiled=True),
    )
    results_part = results_part.astype(jnp.bfloat16)
    return (
        results_part,
        input_part,
        proj_total[None],
        shares[0],
        shares[1],
        shares[2],
        shares[3],
        shares[4].reshape(1, -1),
    )


def solution(mesh):
    return jax.shard_map(
        body,
        mesh=mesh,
        in_specs=(
            P(None, "dp", "section", None),
            P(None, "dp", "section", None),
            P(None, "dp", None),
            P("section", None, None),
            P("section", None),
            P("section", None),
            P("section", None),
            P("section", None),
            P("section", None),
        ),
        out_specs=(
            P(None, "dp", "section", None),
            P(None, "dp", "section", None),
            P("section", None, None),
            P("section", None),
            P("section", None),
            P("section", None),
            P("section", None),
            P("section", None),
        ),
        check_vma=False,
    )
```

profile of v0, /device:TPU:0, one launch (start us, length us, event | category | flops | bytes accessed | tf_op | source)
XLA Modules:
  0.0 1933.8 jit_solution(1698737942374826345)
XLA Ops:
  32.7 10.7 all-gather.3.cloned.1.call-done
  43.4 6.9 copy.204
  50.2 19.0 all-gather.5.cloned.1.call-done
  104.2 469.5 %while.96 = (s32[]{:T(128)}, f32[3,1,1152,512]{2,3,1,0:T(8,128)}, bf16[3,1,1152,8,64]{2,4,3,1,0:T(8,128)(2,1)}, bf16[3,1,1152,8,64]{2,4,3,1,0:T(8,128)(2,1)}, bf...) while((s32[]{:T(128)}, f32[3,1,1152,512]{2,3,1,0:T(8,128)}, ...), condition=%wide.region_26.27_spmd, body=%wide.region_0.26_spmd.sunk | while | flops 9434145792 | bytes 326938752 | solution.py:480
  105.8 96.6 %conditional.5 = (bf16[1,1152,512]{1,2,0:T(8,128)(2,1)}, bf16[1,384,512]{2,1,0:T(8,128)(2,1)}, bf16[1,1152,8,64]{1,3,2,0:T(8,128)(2,1)}, bf16[1,1152,8,64]{1,3,2...) conditional(s32[]{:T(128)} %clamp.10, (s32[]{:T(128)}, ...), branch_computations={%region_1.13_spmd, %region_14.14_spmd, %region_15.23_spmd, %region... | conditional | flops 9434145792 | bytes 236792672 | solution.py:459
  120.4 5.8 copy.161
  168.2 11.1 fusion.25
  235.5 96.5 %conditional.5 = (bf16[1,1152,512]{1,2,0:T(8,128)(2,1)}, bf16[1,384,512]{2,1,0:T(8,128)(2,1)}, bf16[1,1152,8,64]{1,3,2,0:T(8,128)(2,1)}, bf16[1,1152,8,64]{1,3,2...) conditional(s32[]{:T(128)} %clamp.10, (s32[]{:T(128)}, ...), branch_computations={%region_1.13_spmd, %region_14.14_spmd, %region_15.23_spmd, %region... | conditional | flops 9434145792 | bytes 236792672 | solution.py:459
  250.0 5.8 copy.161
  297.7 11.1 fusion.25
  365.1 33.8 %conditional.5 = (bf16[1,1152,512]{1,2,0:T(8,128)(2,1)}, bf16[1,384,512]{2,1,0:T(8,128)(2,1)}, bf16[1,1152,8,64]{1,3,2,0:T(8,128)(2,1)}, bf16[1,1152,8,64]{1,3,2...) conditional(s32[]{:T(128)} %clamp.10, (s32[]{:T(128)}, ...), branch_computations={%region_1.13_spmd, %region_14.14_spmd, %region_15.23_spmd, %region... | conditional | flops 9434145792 | bytes 236792672 | solution.py:459
  420.2 4.2 constant_dynamic-update-slice_fusion.33
  432.1 33.8 %conditional.5 = (bf16[1,1152,512]{1,2,0:T(8,128)(2,1)}, bf16[1,384,512]{2,1,0:T(8,128)(2,1)}, bf16[1,1152,8,64]{1,3,2,0:T(8,128)(2,1)}, bf16[1,1152,8,64]{1,3,2...) conditional(s32[]{:T(128)} %clamp.10, (s32[]{:T(128)}, ...), branch_computations={%region_1.13_spmd, %region_14.14_spmd, %region_15.23_spmd, %region... | conditional | flops 9434145792 | bytes 236792672 | solution.py:459
  502.3 30.1 %conditional.5 = (bf16[1,1152,512]{1,2,0:T(8,128)(2,1)}, bf16[1,384,512]{2,1,0:T(8,128)(2,1)}, bf16[1,1152,8,64]{1,3,2,0:T(8,128)(2,1)}, bf16[1,1152,8,64]{1,3,2...) conditional(s32[]{:T(128)} %clamp.10, (s32[]{:T(128)}, ...), branch_computations={%region_1.13_spmd, %region_14.14_spmd, %region_15.23_spmd, %region... | conditional | flops 9434145792 | bytes 236792672 | solution.py:459
  532.4 9.6 collective-permute-start.2
  590.1 817.9 %while.97 = (s32[]{:T(128)}, f32[512,1536]{1,0:T(8,128)}, f32[512,512]{1,0:T(8,128)}, f32[512,2048]{1,0:T(8,128)}, f32[2048,512]{1,0:T(8,128)}, /*index=5*/f32[2...) while((s32[]{:T(128)}, f32[512,1536]{1,0:T(8,128)}, ...), condition=%wide.region_67.68_spmd.clone, body=%wide.region_28.67_spmd.clone.sunk | while | flops 22263482368 | bytes 802106752 | solution.py:583
  591.6 28.9 %conditional.6 = (f32[512,1536]{1,0:T(8,128)}, f32[512,512]{1,0:T(8,128)}, f32[512,2048]{1,0:T(8,128)}, f32[2048,512]{1,0:T(8,128)}, f32[2,512]{1,0:T(2,128)}, /...) conditional(s32[]{:T(128)} %clamp.11, (s32[]{:T(128)}, ...), branch_computations={%region_29.48_spmd, %region_49.49_spmd, %region_50.64_spmd, %regio... | conditional | flops 22263285760 | bytes 771434560 | solution.py:555
  631.7 31.1 %collective-permute-done.5 = bf16[1,1152,512]{1,2,0:T(8,128)(2,1)S(1)} collective-permute-done((bf16[1,1152,512]{1,2,0:T(8,128)(2,1)}, bf16[1,1152,512]{1,2,0:T(8,128)(2,1)S(1)}, u32[]{:S(2)}, u32[]{:S(2)}) %collective-permute-start.5) | collective-permute-done | bytes 1179680 | tf_op jit(solution)/shard_map/while/body/eval_jaxpr/ppermute | solution.py:13
  666.8 28.1 %conditional.6 = (f32[512,1536]{1,0:T(8,128)}, f32[512,512]{1,0:T(8,128)}, f32[512,2048]{1,0:T(8,128)}, f32[2048,512]{1,0:T(8,128)}, f32[2,512]{1,0:T(2,128)}, /...) conditional(s32[]{:T(128)} %clamp.11, (s32[]{:T(128)}, ...), branch_computations={%region_29.48_spmd, %region_49.49_spmd, %region_50.64_spmd, %regio... | conditional | flops 22263285760 | bytes 771434560 | solution.py:555
  706.1 79.1 %collective-permute-done.5 = bf16[1,1152,512]{1,2,0:T(8,128)(2,1)S(1)} collective-permute-done((bf16[1,1152,512]{1,2,0:T(8,128)(2,1)}, bf16[1,1152,512]{1,2,0:T(8,128)(2,1)S(1)}, u32[]{:S(2)}, u32[]{:S(2)}) %collective-permute-start.5) | collective-permute-done | bytes 1179680 | tf_op jit(solution)/shard_map/while/body/eval_jaxpr/ppermute | solution.py:13
  788.9 27.9 %conditional.6 = (f32[512,1536]{1,0:T(8,128)}, f32[512,512]{1,0:T(8,128)}, f32[512,2048]{1,0:T(8,128)}, f32[2048,512]{1,0:T(8,128)}, f32[2,512]{1,0:T(2,128)}, /...) conditional(s32[]{:T(128)} %clamp.11, (s32[]{:T(128)}, ...), branch_computations={%region_29.48_spmd, %region_49.49_spmd, %region_50.64_spmd, %regio... | conditional | flops 22263285760 | bytes 771434560 | solution.py:555
  828.0 86.1 %collective-permute-done.5 = bf16[1,1152,512]{1,2,0:T(8,128)(2,1)S(1)} collective-permute-done((bf16[1,1152,512]{1,2,0:T(8,128)(2,1)}, bf16[1,1152,512]{1,2,0:T(8,128)(2,1)S(1)}, u32[]{:S(2)}, u32[]{:S(2)}) %collective-permute-start.5) | collective-permute-done | bytes 1179680 | tf_op jit(solution)/shard_map/while/body/eval_jaxpr/ppermute | solution.py:13
  918.1 215.3 %conditional.6 = (f32[512,1536]{1,0:T(8,128)}, f32[512,512]{1,0:T(8,128)}, f32[512,2048]{1,0:T(8,128)}, f32[2048,512]{1,0:T(8,128)}, f32[2,512]{1,0:T(2,128)}, /...) conditional(s32[]{:T(128)} %clamp.11, (s32[]{:T(128)}, ...), branch_computations={%region_29.48_spmd, %region_49.49_spmd, %region_50.64_spmd, %regio... | conditional | flops 22263285760 | bytes 771434560 | solution.py:555
  941.8 9.3 fusion.206
  951.1 10.0 fusion.114
  961.2 6.8 fusion.120
  968.0 6.4 multiply_reduce_fusion.11
  994.4 4.7 multiply_reduce_fusion.8
  999.1 6.8 multiply_reduce_fusion.7
  1006.0 6.5 fusion.171
  1012.4 4.9 scatter-add.31
  1030.4 4.9 scatter-add.10
  1038.3 5.7 fusion.191
  1044.0 10.5 multiply_reduce_fusion.5
  1054.5 5.2 fusion.137
  1059.7 7.6 multiply_reduce_fusion.4
  1067.3 5.2 fusion.146
  1073.7 17.0 multiply_reduce_fusion.2
  1090.7 5.2 fusion.127
  1144.7 14.3 collective-permute-done.5
  1162.8 215.3 %conditional.6 = (f32[512,1536]{1,0:T(8,128)}, f32[512,512]{1,0:T(8,128)}, f32[512,2048]{1,0:T(8,128)}, f32[2048,512]{1,0:T(8,128)}, f32[2,512]{1,0:T(2,128)}, /...) conditional(s32[]{:T(128)} %clamp.11, (s32[]{:T(128)}, ...), branch_computations={%region_29.48_spmd, %region_49.49_spmd, %region_50.64_spmd, %regio... | conditional | flops 22263285760 | bytes 771434560 | solution.py:555
  1186.4 9.3 fusion.206
  1195.8 10.0 fusion.114
  1205.8 6.8 fusion.120
  1212.7 6.5 multiply_reduce_fusion.11
  1239.1 4.9 multiply_reduce_fusion.8
  1244.0 6.8 multiply_reduce_fusion.7
  1250.8 6.5 fusion.171
  1257.3 4.9 scatter-add.31
  1275.2 4.9 scatter-add.10
  1283.1 5.7 fusion.191
  1288.9 10.3 multiply_reduce_fusion.5
  1299.1 5.2 fusion.137
  1304.4 7.6 multiply_reduce_fusion.4
  1311.9 5.2 fusion.146
  1318.4 17.0 multiply_reduce_fusion.2
  1335.4 5.2 fusion.127
  1389.4 14.3 collective-permute-done.5
  1413.0 6.0 slice.840
  1418.9 390.1 %all-reduce.11.cloned.1.call-done = (f32[1,512,1536]{2,1,0:T(8,128)}, f32[512,512]{1,0:T(8,128)}, f32[512,2048]{1,0:T(8,128)}, f32[2048,512]{1,0:T(8,128)}) async-done(((f32[1,512,1536]{2,1,0:T(8,128)}, f32[512,512]{1,0:T(8,128)}, f32[512,2048]{1,0:T(8,128)}, f32[2048,512]{1,0:T(8,128)}), (f32[1,512,1536]{2,1,0:T(8,128)}, f32[512,512]{1,0:T(8,128)}, f32[512,2048]{1,0:T(8,128)}, ...) | async-done | bytes 12582928 | tf_op jit(solution)/shard_map/psum | solution.py:604
  1815.8 4.9 collective-permute-start.12
  1823.6 19.0 all-reduce.7
  1846.6 24.2 %reduce-scatter.3.cloned.1.call-done = f32[2,1,288,512]{3,2,1,0:T(8,128)} async-done(((f32[2,1,1152,512]{3,2,1,0:T(8,128)}), f32[2,1,288,512]{3,2,1,0:T(8,128)}) %reduce-scatter.3.cloned.1.call-update) | async-done | bytes 1179664 | tf_op jit(solution)/shard_map/reduce_scatter | solution.py:625
  1879.1 46.1 %reduce-scatter.5.cloned.1.call-done = f32[2,1,288,512]{3,2,1,0:T(8,128)} async-done(((f32[2,1,1152,512]{3,2,1,0:T(8,128)}), f32[2,1,288,512]{3,2,1,0:T(8,128)}) %reduce-scatter.5.cloned.1.call-update) | async-done | bytes 1179664 | tf_op jit(solution)/shard_map/reduce_scatter | solution.py:628
  (933 shorter events, 678.8 us)
Async XLA Ops:
  7.2 36.2 %all-gather.3.cloned.1.call-start = ((), (), s32[]{:S(2)}) async-start(), calls=%async_computation.2 | async-start | bytes 2949120 | tf_op jit(solution)/shard_map/all_gather | solution.py:387
  9.9 59.3 %all-gather.5.cloned.1.call-start = ((), (), s32[]{:S(2)}) async-start(), calls=%async_computation.4 | async-start | bytes 2949120 | tf_op jit(solution)/shard_map/all_gather | solution.py:388
  10.6 1798.4 %all-reduce.11.cloned.1.call-start = ((), (), s32[]{:S(2)}) async-start(), calls=%async_computation.6 | async-start | bytes 25165824 | tf_op jit(solution)/shard_map/psum | solution.py:604
  10.7 18.6 collective-permute-start.10
  12.0 10.8 collective-permute-start.7
  13.3 14.3 collective-permute-start.8
  14.6 15.7 collective-permute-start.9
  21.5 5.5 collective-permute-start.6
  128.4 24.3 %copy-start.44 = (bf16[1,1152,8,64]{1,3,2,0:T(8,128)(2,1)}, bf16[1,1152,8,64]{1,3,2,0:T(8,128)(2,1)S(1)}, u32[]{:S(2)}) copy-start(bf16[1,1152,8,64]{1,3,2,0:T(8,128)(2,1)S(1)} %get-tuple-element.3150) | copy-start | bytes 3538948 | tf_op jit(solution)/shard_map/while/body/eval_jaxpr/cond
  128.4 24.3 %copy-start.46 = (bf16[1,1152,8,64]{1,3,2,0:T(8,128)(2,1)}, bf16[1,1152,8,64]{1,3,2,0:T(8,128)(2,1)S(1)}, u32[]{:S(2)}) copy-start(bf16[1,1152,8,64]{1,3,2,0:T(8,128)(2,1)S(1)} %get-tuple-element.3149) | copy-start | bytes 3538948 | tf_op jit(solution)/shard_map/while/body/eval_jaxpr/cond
  128.4 30.2 %copy-start.56 = (bf16[1,1152,8,64]{1,3,2,0:T(8,128)(2,1)}, bf16[1,1152,8,64]{1,3,2,0:T(8,128)(2,1)S(1)}, u32[]{:S(2)}) copy-start(bf16[1,1152,8,64]{1,3,2,0:T(8,128)(2,1)S(1)} %get-tuple-element.3151) | copy-start | bytes 3538948 | tf_op jit(solution)/shard_map/while/body/eval_jaxpr/cond
  202.4 29.1 %collective-permute-start.2 = (bf16[1,1152,512]{1,2,0:T(8,128)(2,1)}, bf16[1,1152,512]{1,2,0:T(8,128)(2,1)}, u32[]{:S(2)}, u32[]{:S(2)}) collective-permute-start(bf16[1,1152,512]{1,2,0:T(8,128)(2,1)} %get-tuple-element.3096), channel_id=1, source_target_pairs={{0,24},{1,25},{2,26},{3,27},{4,28},{5,29},{6,30},{7,31}} | collective-permute-start | bytes 3538952 | tf_op jit(solution)/shard_map/while/body/eval_jaxpr/ppermute | solution.py:13
  204.8 29.1 %collective-permute-start = (bf16[1,1152,512]{1,2,0:T(8,128)(2,1)}, bf16[1,1152,512]{1,2,0:T(8,128)(2,1)}, u32[]{:S(2)}, u32[]{:S(2)}) collective-permute-start(bf16[1,1152,512]{1,2,0:T(8,128)(2,1)} %get-tuple-element.3096), channel_id=1, source_target_pairs={{0,8},{8,16},{16,24},{1,9},{9,17},{17,25},{2,10},{10,18},{18,26},{... | collective-permute-start | bytes 3538952 | tf_op jit(solution)/shard_map/while/body/eval_jaxpr/ppermute | solution.py:13
  207.1 26.8 %collective-permute-start.1 = (bf16[1,384,512]{2,1,0:T(8,128)(2,1)}, bf16[1,384,512]{2,1,0:T(8,128)(2,1)S(1)}, u32[]{:S(2)}, u32[]{:S(2)}) collective-permute-start(bf16[1,384,512]{2,1,0:T(8,128)(2,1)} %get-tuple-element.3097), channel_id=1, source_target_pairs={{0,8},{8,16},{16,24},{1,9},{9,17},{17,25},{2,10},{10,18},{18,26},{... | collective-permute-start | bytes 1179656 | tf_op jit(solution)/shard_map/while/body/eval_jaxpr/ppermute | solution.py:13
  258.1 24.1 %copy-start.44 = (bf16[1,1152,8,64]{1,3,2,0:T(8,128)(2,1)}, bf16[1,1152,8,64]{1,3,2,0:T(8,128)(2,1)S(1)}, u32[]{:S(2)}) copy-start(bf16[1,1152,8,64]{1,3,2,0:T(8,128)(2,1)S(1)} %get-tuple-element.3150) | copy-start | bytes 3538948 | tf_op jit(solution)/shard_map/while/body/eval_jaxpr/cond
  258.1 24.1 %copy-start.46 = (bf16[1,1152,8,64]{1,3,2,0:T(8,128)(2,1)}, bf16[1,1152,8,64]{1,3,2,0:T(8,128)(2,1)S(1)}, u32[]{:S(2)}) copy-start(bf16[1,1152,8,64]{1,3,2,0:T(8,128)(2,1)S(1)} %get-tuple-element.3149) | copy-start | bytes 3538948 | tf_op jit(solution)/shard_map/while/body/eval_jaxpr/cond
  258.1 30.1 %copy-start.56 = (bf16[1,1152,8,64]{1,3,2,0:T(8,128)(2,1)}, bf16[1,1152,8,64]{1,3,2,0:T(8,128)(2,1)S(1)}, u32[]{:S(2)}) copy-start(bf16[1,1152,8,64]{1,3,2,0:T(8,128)(2,1)S(1)} %get-tuple-element.3151) | copy-start | bytes 3538948 | tf_op jit(solution)/shard_map/while/body/eval_jaxpr/cond
  331.9 29.2 %collective-permute-start.2 = (bf16[1,1152,512]{1,2,0:T(8,128)(2,1)}, bf16[1,1152,512]{1,2,0:T(8,128)(2,1)}, u32[]{:S(2)}, u32[]{:S(2)}) collective-permute-start(bf16[1,1152,512]{1,2,0:T(8,128)(2,1)} %get-tuple-element.3096), channel_id=1, source_target_pairs={{0,24},{1,25},{2,26},{3,27},{4,28},{5,29},{6,30},{7,31}} | collective-permute-start | bytes 3538952 | tf_op jit(solution)/shard_map/while/body/eval_jaxpr/ppermute | solution.py:13
  334.3 29.2 %collective-permute-start = (bf16[1,1152,512]{1,2,0:T(8,128)(2,1)}, bf16[1,1152,512]{1,2,0:T(8,128)(2,1)}, u32[]{:S(2)}, u32[]{:S(2)}) collective-permute-start(bf16[1,1152,512]{1,2,0:T(8,128)(2,1)} %get-tuple-element.3096), channel_id=1, source_target_pairs={{0,8},{8,16},{16,24},{1,9},{9,17},{17,25},{2,10},{10,18},{18,26},{... | collective-permute-start | bytes 3538952 | tf_op jit(solution)/shard_map/while/body/eval_jaxpr/ppermute | solution.py:13
  336.6 26.8 %collective-permute-start.1 = (bf16[1,384,512]{2,1,0:T(8,128)(2,1)}, bf16[1,384,512]{2,1,0:T(8,128)(2,1)S(1)}, u32[]{:S(2)}, u32[]{:S(2)}) collective-permute-start(bf16[1,384,512]{2,1,0:T(8,128)(2,1)} %get-tuple-element.3097), channel_id=1, source_target_pairs={{0,8},{8,16},{16,24},{1,9},{9,17},{17,25},{2,10},{10,18},{18,26},{... | collective-permute-start | bytes 1179656 | tf_op jit(solution)/shard_map/while/body/eval_jaxpr/ppermute | solution.py:13
  398.9 29.2 %collective-permute-start.2 = (bf16[1,1152,512]{1,2,0:T(8,128)(2,1)}, bf16[1,1152,512]{1,2,0:T(8,128)(2,1)}, u32[]{:S(2)}, u32[]{:S(2)}) collective-permute-start(bf16[1,1152,512]{1,2,0:T(8,128)(2,1)} %get-tuple-element.3096), channel_id=1, source_target_pairs={{0,24},{1,25},{2,26},{3,27},{4,28},{5,29},{6,30},{7,31}} | collective-permute-start | bytes 3538952 | tf_op jit(solution)/shard_map/while/body/eval_jaxpr/ppermute | solution.py:13
  401.3 29.2 %collective-permute-start = (bf16[1,1152,512]{1,2,0:T(8,128)(2,1)}, bf16[1,1152,512]{1,2,0:T(8,128)(2,1)}, u32[]{:S(2)}, u32[]{:S(2)}) collective-permute-start(bf16[1,1152,512]{1,2,0:T(8,128)(2,1)} %get-tuple-element.3096), channel_id=1, source_target_pairs={{0,8},{8,16},{16,24},{1,9},{9,17},{17,25},{2,10},{10,18},{18,26},{... | collective-permute-start | bytes 3538952 | tf_op jit(solution)/shard_map/while/body/eval_jaxpr/ppermute | solution.py:13
  403.6 26.9 %collective-permute-start.1 = (bf16[1,384,512]{2,1,0:T(8,128)(2,1)}, bf16[1,384,512]{2,1,0:T(8,128)(2,1)S(1)}, u32[]{:S(2)}, u32[]{:S(2)}) collective-permute-start(bf16[1,384,512]{2,1,0:T(8,128)(2,1)} %get-tuple-element.3097), channel_id=1, source_target_pairs={{0,8},{8,16},{16,24},{1,9},{9,17},{17,25},{2,10},{10,18},{18,26},{... | collective-permute-start | bytes 1179656 | tf_op jit(solution)/shard_map/while/body/eval_jaxpr/ppermute | solution.py:13
  465.9 32.4 %collective-permute-start.2 = (bf16[1,1152,512]{1,2,0:T(8,128)(2,1)}, bf16[1,1152,512]{1,2,0:T(8,128)(2,1)}, u32[]{:S(2)}, u32[]{:S(2)}) collective-permute-start(bf16[1,1152,512]{1,2,0:T(8,128)(2,1)} %get-tuple-element.3096), channel_id=1, source_target_pairs={{0,24},{1,25},{2,26},{3,27},{4,28},{5,29},{6,30},{7,31}} | collective-permute-start | bytes 3538952 | tf_op jit(solution)/shard_map/while/body/eval_jaxpr/ppermute | solution.py:13
  469.6 31.1 %collective-permute-start = (bf16[1,1152,512]{1,2,0:T(8,128)(2,1)}, bf16[1,1152,512]{1,2,0:T(8,128)(2,1)}, u32[]{:S(2)}, u32[]{:S(2)}) collective-permute-start(bf16[1,1152,512]{1,2,0:T(8,128)(2,1)} %get-tuple-element.3096), channel_id=1, source_target_pairs={{0,8},{8,16},{16,24},{1,9},{9,17},{17,25},{2,10},{10,18},{18,26},{... | collective-permute-start | bytes 3538952 | tf_op jit(solution)/shard_map/while/body/eval_jaxpr/ppermute | solution.py:13
  471.9 28.8 %collective-permute-start.1 = (bf16[1,384,512]{2,1,0:T(8,128)(2,1)}, bf16[1,384,512]{2,1,0:T(8,128)(2,1)S(1)}, u32[]{:S(2)}, u32[]{:S(2)}) collective-permute-start(bf16[1,384,512]{2,1,0:T(8,128)(2,1)} %get-tuple-element.3097), channel_id=1, source_target_pairs={{0,8},{8,16},{16,24},{1,9},{9,17},{17,25},{2,10},{10,18},{18,26},{... | collective-permute-start | bytes 1179656 | tf_op jit(solution)/shard_map/while/body/eval_jaxpr/ppermute | solution.py:13
  532.4 36.4 %collective-permute-start.2 = (bf16[1,1152,512]{1,2,0:T(8,128)(2,1)}, bf16[1,1152,512]{1,2,0:T(8,128)(2,1)}, u32[]{:S(2)}, u32[]{:S(2)}) collective-permute-start(bf16[1,1152,512]{1,2,0:T(8,128)(2,1)} %get-tuple-element.3096), channel_id=1, source_target_pairs={{0,24},{1,25},{2,26},{3,27},{4,28},{5,29},{6,30},{7,31}} | collective-permute-start | bytes 3538952 | tf_op jit(solution)/shard_map/while/body/eval_jaxpr/ppermute | solution.py:13
  542.0 29.2 %collective-permute-start = (bf16[1,1152,512]{1,2,0:T(8,128)(2,1)}, bf16[1,1152,512]{1,2,0:T(8,128)(2,1)}, u32[]{:S(2)}, u32[]{:S(2)}) collective-permute-start(bf16[1,1152,512]{1,2,0:T(8,128)(2,1)} %get-tuple-element.3096), channel_id=1, source_target_pairs={{0,8},{8,16},{16,24},{1,9},{9,17},{17,25},{2,10},{10,18},{18,26},{... | collective-permute-start | bytes 3538952 | tf_op jit(solution)/shard_map/while/body/eval_jaxpr/ppermute | solution.py:13
  544.3 26.9 %collective-permute-start.1 = (bf16[1,384,512]{2,1,0:T(8,128)(2,1)}, bf16[1,384,512]{2,1,0:T(8,128)(2,1)S(1)}, u32[]{:S(2)}, u32[]{:S(2)}) collective-permute-start(bf16[1,384,512]{2,1,0:T(8,128)(2,1)} %get-tuple-element.3097), channel_id=1, source_target_pairs={{0,8},{8,16},{16,24},{1,9},{9,17},{17,25},{2,10},{10,18},{18,26},{... | collective-permute-start | bytes 1179656 | tf_op jit(solution)/shard_map/while/body/eval_jaxpr/ppermute | solution.py:13
  620.5 43.5 %collective-permute-start.3 = (f32[1,1152,512]{2,1,0:T(8,128)}, f32[1,1152,512]{2,1,0:T(8,128)}, u32[]{:S(2)}, u32[]{:S(2)}) collective-permute-start(f32[1,1152,512]{2,1,0:T(8,128)} %get-tuple-element.3144), channel_id=1, source_target_pairs={{8,0},{16,8},{24,16},{9,1},{17,9},{25,17},{10,2},{18,10},{26,18},{... | collective-permute-start | bytes 7077896 | tf_op jit(solution)/shard_map/while/body/eval_jaxpr/ppermute | solution.py:13
  624.2 38.7 %collective-permute-start.5 = (bf16[1,1152,512]{1,2,0:T(8,128)(2,1)}, bf16[1,1152,512]{1,2,0:T(8,128)(2,1)S(1)}, u32[]{:S(2)}, u32[]{:S(2)}) collective-permute-start(bf16[1,1152,512]{1,2,0:T(8,128)(2,1)} %copy.236), channel_id=1, source_target_pairs={{24,0},{25,1},{26,2},{27,3},{28,4},{29,5},{30,6},{31,7}} | collective-permute-start | bytes 3538952 | tf_op jit(solution)/shard_map/while/body/eval_jaxpr/ppermute | solution.py:13
  625.5 38.5 %collective-permute-start.4 = (bf16[1,384,512]{2,1,0:T(8,128)(2,1)}, bf16[1,384,512]{2,1,0:T(8,128)(2,1)}, u32[]{:S(2)}, u32[]{:S(2)}) collective-permute-start(bf16[1,384,512]{2,1,0:T(8,128)(2,1)} %get-tuple-element.3145), channel_id=1, source_target_pairs={{8,0},{16,8},{24,16},{9,1},{17,9},{25,17},{10,2},{18,10},{26,18},{... | collective-permute-start | bytes 1179656 | tf_op jit(solution)/shard_map/while/body/eval_jaxpr/ppermute | solution.py:13
  631.7 32.3 %copy-start.116 = (s32[5]{0:T(128)S(1)}, s32[5]{0:T(128)}, u32[]{:S(2)}) copy-start(s32[5]{0:T(128)} %copy-done.115) | copy-start | bytes 64 | tf_op jit(solution)/shard_map/while
  694.9 91.5 %collective-permute-start.3 = (f32[1,1152,512]{2,1,0:T(8,128)}, f32[1,1152,512]{2,1,0:T(8,128)}, u32[]{:S(2)}, u32[]{:S(2)}) collective-permute-start(f32[1,1152,512]{2,1,0:T(8,128)} %get-tuple-element.3144), channel_id=1, source_target_pairs={{8,0},{16,8},{24,16},{9,1},{17,9},{25,17},{10,2},{18,10},{26,18},{... | collective-permute-start | bytes 7077896 | tf_op jit(solution)/shard_map/while/body/eval_jaxpr/ppermute | solution.py:13
  698.6 86.6 %collective-permute-start.5 = (bf16[1,1152,512]{1,2,0:T(8,128)(2,1)}, bf16[1,1152,512]{1,2,0:T(8,128)(2,1)S(1)}, u32[]{:S(2)}, u32[]{:S(2)}) collective-permute-start(bf16[1,1152,512]{1,2,0:T(8,128)(2,1)} %copy.236), channel_id=1, source_target_pairs={{24,0},{25,1},{26,2},{27,3},{28,4},{29,5},{30,6},{31,7}} | collective-permute-start | bytes 3538952 | tf_op jit(solution)/shard_map/while/body/eval_jaxpr/ppermute | solution.py:13
  699.9 86.5 %collective-permute-start.4 = (bf16[1,384,512]{2,1,0:T(8,128)(2,1)}, bf16[1,384,512]{2,1,0:T(8,128)(2,1)}, u32[]{:S(2)}, u32[]{:S(2)}) collective-permute-start(bf16[1,384,512]{2,1,0:T(8,128)(2,1)} %get-tuple-element.3145), channel_id=1, source_target_pairs={{8,0},{16,8},{24,16},{9,1},{17,9},{25,17},{10,2},{18,10},{26,18},{... | collective-permute-start | bytes 1179656 | tf_op jit(solution)/shard_map/while/body/eval_jaxpr/ppermute | solution.py:13
  706.1 80.2 %copy-start.116 = (s32[5]{0:T(128)S(1)}, s32[5]{0:T(128)}, u32[]{:S(2)}) copy-start(s32[5]{0:T(128)} %copy-done.115) | copy-start | bytes 64 | tf_op jit(solution)/shard_map/while
  816.8 98.5 %collective-permute-start.3 = (f32[1,1152,512]{2,1,0:T(8,128)}, f32[1,1152,512]{2,1,0:T(8,128)}, u32[]{:S(2)}, u32[]{:S(2)}) collective-permute-start(f32[1,1152,512]{2,1,0:T(8,128)} %get-tuple-element.3144), channel_id=1, source_target_pairs={{8,0},{16,8},{24,16},{9,1},{17,9},{25,17},{10,2},{18,10},{26,18},{... | collective-permute-start | bytes 7077896 | tf_op jit(solution)/shard_map/while/body/eval_jaxpr/ppermute | solution.py:13
  820.5 93.6 %collective-permute-start.5 = (bf16[1,1152,512]{1,2,0:T(8,128)(2,1)}, bf16[1,1152,512]{1,2,0:T(8,128)(2,1)S(1)}, u32[]{:S(2)}, u32[]{:S(2)}) collective-permute-start(bf16[1,1152,512]{1,2,0:T(8,128)(2,1)} %copy.236), channel_id=1, source_target_pairs={{24,0},{25,1},{26,2},{27,3},{28,4},{29,5},{30,6},{31,7}} | collective-permute-start | bytes 3538952 | tf_op jit(solution)/shard_map/while/body/eval_jaxpr/ppermute | solution.py:13
  821.8 93.5 %collective-permute-start.4 = (bf16[1,384,512]{2,1,0:T(8,128)(2,1)}, bf16[1,384,512]{2,1,0:T(8,128)(2,1)}, u32[]{:S(2)}, u32[]{:S(2)}) collective-permute-start(bf16[1,384,512]{2,1,0:T(8,128)(2,1)} %get-tuple-element.3145), channel_id=1, source_target_pairs={{8,0},{16,8},{24,16},{9,1},{17,9},{25,17},{10,2},{18,10},{26,18},{... | collective-permute-start | bytes 1179656 | tf_op jit(solution)/shard_map/while/body/eval_jaxpr/ppermute | solution.py:13
  828.0 87.3 %copy-start.116 = (s32[5]{0:T(128)S(1)}, s32[5]{0:T(128)}, u32[]{:S(2)}) copy-start(s32[5]{0:T(128)} %copy-done.115) | copy-start | bytes 64 | tf_op jit(solution)/shard_map/while
  941.5 45.8 %copy-start.35 = (bf16[1,1152,8,64]{1,3,2,0:T(8,128)(2,1)}, bf16[1,1152,8,64]{1,3,2,0:T(8,128)(2,1)S(1)}, u32[]{:S(2)}) copy-start(bf16[1,1152,8,64]{1,3,2,0:T(8,128)(2,1)S(1)} %get-tuple-element.2619) | copy-start | bytes 3538948 | tf_op jit(solution)/shard_map/while/body/eval_jaxpr/cond
  941.5 52.9 %copy-start.17 = (bf16[1,1152,8,64]{1,3,2,0:T(8,128)(2,1)}, bf16[1,1152,8,64]{1,3,2,0:T(8,128)(2,1)S(1)}, u32[]{:S(2)}) copy-start(bf16[1,1152,8,64]{1,3,2,0:T(8,128)(2,1)S(1)} %get-tuple-element.2620) | copy-start | bytes 3538948 | tf_op jit(solution)/shard_map/while/body/eval_jaxpr/cond
  941.8 26.2 %slice-start.2 = ((s8[7077888]{0:T(1024)(128)(4,1)}), s8[4194304]{0:T(1024)(128)(4,1)S(1)}, s32[]{:S(2)}) async-start(s8[7077888]{0:T(1024)(128)(4,1)} %bitcast.701), calls=%async_computation.9 | async-start | bytes 8388608 | tf_op jit(solution)/shard_map/while/body/eval_jaxpr/cond
  951.1 16.8 slice-start.3
  1133.4 26.8 %collective-permute-start.3 = (f32[1,1152,512]{2,1,0:T(8,128)}, f32[1,1152,512]{2,1,0:T(8,128)}, u32[]{:S(2)}, u32[]{:S(2)}) collective-permute-start(f32[1,1152,512]{2,1,0:T(8,128)} %get-tuple-element.3144), channel_id=1, source_target_pairs={{8,0},{16,8},{24,16},{9,1},{17,9},{25,17},{10,2},{18,10},{26,18},{... | collective-permute-start | bytes 7077896 | tf_op jit(solution)/shard_map/while/body/eval_jaxpr/ppermute | solution.py:13
  1137.1 21.9 %collective-permute-start.5 = (bf16[1,1152,512]{1,2,0:T(8,128)(2,1)}, bf16[1,1152,512]{1,2,0:T(8,128)(2,1)S(1)}, u32[]{:S(2)}, u32[]{:S(2)}) collective-permute-start(bf16[1,1152,512]{1,2,0:T(8,128)(2,1)} %copy.236), channel_id=1, source_target_pairs={{24,0},{25,1},{26,2},{27,3},{28,4},{29,5},{30,6},{31,7}} | collective-permute-start | bytes 3538952 | tf_op jit(solution)/shard_map/while/body/eval_jaxpr/ppermute | solution.py:13
  1138.4 21.8 %collective-permute-start.4 = (bf16[1,384,512]{2,1,0:T(8,128)(2,1)}, bf16[1,384,512]{2,1,0:T(8,128)(2,1)}, u32[]{:S(2)}, u32[]{:S(2)}) collective-permute-start(bf16[1,384,512]{2,1,0:T(8,128)(2,1)} %get-tuple-element.3145), channel_id=1, source_target_pairs={{8,0},{16,8},{24,16},{9,1},{17,9},{25,17},{10,2},{18,10},{26,18},{... | collective-permute-start | bytes 1179656 | tf_op jit(solution)/shard_map/while/body/eval_jaxpr/ppermute | solution.py:13
  1144.7 15.5 copy-start.116
  1186.2 45.9 %copy-start.35 = (bf16[1,1152,8,64]{1,3,2,0:T(8,128)(2,1)}, bf16[1,1152,8,64]{1,3,2,0:T(8,128)(2,1)S(1)}, u32[]{:S(2)}) copy-start(bf16[1,1152,8,64]{1,3,2,0:T(8,128)(2,1)S(1)} %get-tuple-element.2619) | copy-start | bytes 3538948 | tf_op jit(solution)/shard_map/while/body/eval_jaxpr/cond
  1186.2 53.0 %copy-start.17 = (bf16[1,1152,8,64]{1,3,2,0:T(8,128)(2,1)}, bf16[1,1152,8,64]{1,3,2,0:T(8,128)(2,1)S(1)}, u32[]{:S(2)}) copy-start(bf16[1,1152,8,64]{1,3,2,0:T(8,128)(2,1)S(1)} %get-tuple-element.2620) | copy-start | bytes 3538948 | tf_op jit(solution)/shard_map/while/body/eval_jaxpr/cond
  1186.4 26.2 %slice-start.2 = ((s8[7077888]{0:T(1024)(128)(4,1)}), s8[4194304]{0:T(1024)(128)(4,1)S(1)}, s32[]{:S(2)}) async-start(s8[7077888]{0:T(1024)(128)(4,1)} %bitcast.701), calls=%async_computation.9 | async-start | bytes 8388608 | tf_op jit(solution)/shard_map/while/body/eval_jaxpr/cond
  1195.8 16.9 slice-start.3
  1378.1 26.8 %collective-permute-start.3 = (f32[1,1152,512]{2,1,0:T(8,128)}, f32[1,1152,512]{2,1,0:T(8,128)}, u32[]{:S(2)}, u32[]{:S(2)}) collective-permute-start(f32[1,1152,512]{2,1,0:T(8,128)} %get-tuple-element.3144), channel_id=1, source_target_pairs={{8,0},{16,8},{24,16},{9,1},{17,9},{25,17},{10,2},{18,10},{26,18},{... | collective-permute-start | bytes 7077896 | tf_op jit(solution)/shard_map/while/body/eval_jaxpr/ppermute | solution.py:13
  1381.8 21.9 %collective-permute-start.5 = (bf16[1,1152,512]{1,2,0:T(8,128)(2,1)}, bf16[1,1152,512]{1,2,0:T(8,128)(2,1)S(1)}, u32[]{:S(2)}, u32[]{:S(2)}) collective-permute-start(bf16[1,1152,512]{1,2,0:T(8,128)(2,1)} %copy.236), channel_id=1, source_target_pairs={{24,0},{25,1},{26,2},{27,3},{28,4},{29,5},{30,6},{31,7}} | collective-permute-start | bytes 3538952 | tf_op jit(solution)/shard_map/while/body/eval_jaxpr/ppermute | solution.py:13
  1383.1 21.8 %collective-permute-start.4 = (bf16[1,384,512]{2,1,0:T(8,128)(2,1)}, bf16[1,384,512]{2,1,0:T(8,128)(2,1)}, u32[]{:S(2)}, u32[]{:S(2)}) collective-permute-start(bf16[1,384,512]{2,1,0:T(8,128)(2,1)} %get-tuple-element.3145), channel_id=1, source_target_pairs={{8,0},{16,8},{24,16},{9,1},{17,9},{25,17},{10,2},{18,10},{26,18},{... | collective-permute-start | bytes 1179656 | tf_op jit(solution)/shard_map/while/body/eval_jaxpr/ppermute | solution.py:13
  1408.1 462.8 %reduce-scatter.3.cloned.1.call-start = ((), (), s32[]{:S(2)}) async-start(), calls=%async_computation.3 | async-start | bytes 5898240 | tf_op jit(solution)/shard_map/reduce_scatter | solution.py:625
  1412.9 512.2 %reduce-scatter.5.cloned.1.call-start = ((), (), s32[]{:S(2)}) async-start(), calls=%async_computation.5 | async-start | bytes 5898240 | tf_op jit(solution)/shard_map/reduce_scatter | solution.py:628
  1812.3 61.6 %collective-permute-start.13 = (f32[1024,512]{1,0:T(8,128)}, f32[1024,512]{1,0:T(8,128)S(1)}, u32[]{:S(2)}, u32[]{:S(2)}) collective-permute-start(f32[1024,512]{1,0:T(8,128)} %slice.925), channel_id=1, source_target_pairs={{0,8},{8,16},{16,24},{1,9},{9,17},{17,25},{2,10},{10,18},{18,26},{... | collective-permute-start | bytes 6291464 | tf_op jit(solution)/shard_map/ppermute | solution.py:13
  1815.8 61.7 %collective-permute-start.12 = (f32[256,2048]{1,0:T(8,128)}, f32[256,2048]{1,0:T(8,128)}, u32[]{:S(2)}, u32[]{:S(2)}) collective-permute-start(f32[256,2048]{1,0:T(8,128)} %slice.923), channel_id=1, source_target_pairs={{0,8},{8,16},{16,24},{1,9},{9,17},{17,25},{2,10},{10,18},{18,26},{... | collective-permute-start | bytes 6291464 | tf_op jit(solution)/shard_map/ppermute | solution.py:13
  1821.5 51.5 %collective-permute-start.11 = (f32[256,512]{1,0:T(8,128)}, f32[256,512]{1,0:T(8,128)}, u32[]{:S(2)}, u32[]{:S(2)}) collective-permute-start(f32[256,512]{1,0:T(8,128)} %slice.921), channel_id=1, source_target_pairs={{0,8},{8,16},{16,24},{1,9},{9,17},{17,25},{2,10},{10,18},{18,26},{... | collective-permute-start | bytes 1572872 | tf_op jit(solution)/shard_map/ppermute | solution.py:13
  1842.6 2.6 collective-permute-start.15
  1843.9 2.1 collective-permute-start.14
  1877.4 47.7 %copy-start.90 = (f32[1,512,1536]{2,1,0:T(8,128)S(1)}, f32[1,512,1536]{2,1,0:T(8,128)}, u32[]{:S(2)}) copy-start(f32[1,512,1536]{2,1,0:T(8,128)} %get-tuple-element.3537) | copy-start | bytes 9437188
  (180 other events, 692.7 us)
Sparse Core Ops, SparseCore 0:
  10.2 33.1 all-gather.2
  44.9 24.2 all-gather.4
  1408.2 400.8 all-reduce.10
  1811.6 59.1 reduce-scatter.2
  1873.8 51.3 reduce-scatter.4
where the time goes:
time: 1940 us; the launch traced here: 1930 us
  waiting for transfers between devices  719 us (37%)
  local copies, waits for them, and re-layouts  423 us (22%)
  matrix products  329 us (17%)
  loops' own time  208 us (11%)
  other arithmetic  144 us (7%)
  starting transfers between devices  77.8 us (4%)
    psum x1, waiting for transfers between devices, body(): summed = lax.psum((proj_grad,) + tuple(block_grads), 'dp')  390 us
    ppermute x40, waiting for transfers between devices, passed_along(): lax.ppermute(value, axis, [(source, source + steps) for source in range(f...  228 us
    dynamic_update_slice x80, local copies, waits for them, and re-layouts, store_one(): lax.dynamic_update_index_in_dim(whole_buf, piece_val.astype(whole_buf.dty...  135 us
    another operation x5, loops' own time, backward_tick(): lax.switch(branch_index, [backward_one, backward_two, backward_three, bac...  103 us
    another operation x58, local copies, waits for them, and re-layouts  82 us
    ppermute x40, starting transfers between devices, passed_along(): lax.ppermute(value, axis, [(source, source + steps) for source in range(f...  77.6 us
    another operation x5, loops' own time, forward_tick(): lax.switch(branch_index, [forward_one, forward_two, forward_three, forwar...  75.8 us
    dot_general x16, matrix products, block_scores(): jnp.einsum('bqhd,bkhd->bhqk', queries[:, row_start:row_stop, head_start:h...  75.6 us
  transfers between devices with their start and end apart: 45, of which 12 were waited for; matrix products, arithmetic and copies ran while one was open for 10% of the time, Pallas kernels for 0%

commit v1 on v0

v1 whole, which is shorter than its diff:
```python
import functools

import jax
import jax.numpy as jnp
from jax import lax
from jax.experimental import pallas as pl
from jax.experimental.pallas import tpu as pltpu
from jax.sharding import PartitionSpec as P

EPSILON = 1e-05
APART = -1e30
F32 = jnp.float32
BF16 = jnp.bfloat16
VMEM_LIMIT = 60 * 1024 * 1024
LANES = 128
PARTS = 4
HALF = 64
MESH = pl.DeviceIdType.MESH


def dot(left, right, left_dim, right_dim):
    return lax.dot_general(
        left, right, (((left_dim,), (right_dim,)), ((), ())), preferred_element_type=F32
    )


def standardize(value):
    centred = value - jnp.mean(value, axis=-1, keepdims=True)
    inverse = lax.rsqrt(jnp.mean(centred * centred, axis=-1, keepdims=True) + EPSILON)
    return centred * inverse, inverse


def norm_back(grad, gain, standard, inverse):
    scaled = grad * gain
    centred = (
        scaled
        - jnp.mean(scaled, axis=-1, keepdims=True)
        - standard * jnp.mean(scaled * standard, axis=-1, keepdims=True)
    )
    return centred * inverse


def params(limit=VMEM_LIMIT):
    return pltpu.CompilerParams(vmem_limit_bytes=limit)


def row_cuts(length, step):
    return [slice(start, start + step) for start in range(0, length, step)]


def lane_ids(rows):
    return lax.broadcasted_iota(jnp.int32, (rows, LANES), 1)


def barrier_with(devices):
    barrier = pltpu.get_barrier_semaphore()
    for device in devices:
        pl.semaphore_signal(barrier, inc=1, device_id=device, device_id_type=MESH)
    pl.semaphore_wait(barrier, len(devices))


def make_marks(wide, lane):
    length = wide.shape[0]
    mark = lane % HALF
    position = lax.broadcasted_iota(jnp.int32, (length, LANES), 0)
    low = position % 256
    same = wide == (mark - 2).astype(F32)
    chosen = (mark >= 2) & (mark < 5)
    query = jnp.where(chosen & same, 1.0, 0.0)
    fixed = jnp.where(mark < 8, 1.0, 0.0)
    apart = jnp.where(same, 0.0, APART)
    key = jnp.where(chosen, apart, fixed)
    key = jnp.where(mark == 0, low.astype(F32), key)
    key = jnp.where(mark == 1, (position - low).astype(F32), key)
    return query.astype(BF16), key.astype(BF16)


def gelu_pieces(value):
    root = 0.7978845608028654
    square = value * value
    inner = jnp.tanh(value * (root + (root * 0.044715) * square))
    half = 0.5 + 0.5 * inner
    active = value * half
    slant = half + active * (1.0 - inner) * (root + (3.0 * root * 0.044715) * square)
    return active, slant


LINE = 4
SQUARE = 2 * LINE


def head_back(
    side,
    key_mark_ref,
    query_ref,
    key_ref,
    value_ref,
    attended_ref,
    attended_grad_ref,
    mixed,
    keys,
    values,
    grads,
    key_sum,
    value_sum,
    cuts,
    tile,
):
    length = key_ref.shape[0]
    blocks = length // tile
    lane = lane_ids(tile)
    here = lane // HALF == side
    mark = lane % HALF
    earlier = lax.broadcasted_iota(jnp.int32, (tile, tile), 0) <= lax.broadcasted_iota(
        jnp.int32, (tile, tile), 1
    )
    position = lax.broadcasted_iota(jnp.int32, (tile, LANES), 0)
    spans = [slice(block * tile, (block + 1) * tile) for block in range(blocks)]
    for rows in spans:
        grad = attended_grad_ref[rows, :].astype(F32)
        product = jnp.where(here, grad * attended_ref[rows, :].astype(F32), 0.0)
        keys[rows, :] = jnp.where(
            here, key_ref[rows, :].astype(F32), key_mark_ref[rows, :].astype(F32)
        ).astype(BF16)
        values[rows, :] = jnp.where(here, value_ref[rows, :].astype(F32), 1.0).astype(BF16)
        centre = -jnp.sum(product, axis=1, keepdims=True)
        first = centre.astype(BF16).astype(F32)
        second = (centre - first).astype(BF16).astype(F32)
        third = centre - first - second
        marks = jnp.where(
            mark == 0, first, jnp.where(mark == 1, second, jnp.where(mark == 2, third, 0.0))
        )
        grads[rows, :] = jnp.where(here, grad, marks).astype(BF16)

    def score(block, other):
        rows, cols = spans[block], spans[other]
        raw = dot(keys[cols, :], query_ref[0, rows, :], 1, 1)
        return raw, dot(values[cols, :], grads[rows, :], 1, 1)

    def finish(block, other, raw, pull):
        rows, cols = spans[block], spans[other]
        weights = jnp.exp(raw)
        if other == block:
            weights = jnp.where(earlier, weights, 0.0)
        change = (weights * pull).astype(BF16)
        key_term = dot(change, query_ref[0, rows, :], 1, 0)
        value_term = dot(weights.astype(BF16), grads[rows, :], 1, 0)
        if other == block:
            key_sum[cols, :] = key_term
            value_sum[cols, :] = value_term
        else:
            key_sum[cols, :] += key_term
            value_sum[cols, :] += value_term
        return dot(change, keys[cols, :], 0, 0)

    def keep(rows, cut, value):
        mixed[rows, cut] = jnp.where(here, value, mixed[rows, cut].astype(F32)).astype(BF16)

    order = [(block, other) for block in range(blocks) for other in range(block + 1)]
    ahead = score(*order[0])
    slope_sum = jnp.zeros((tile, LANES), F32)
    total = None
    for index, (block, other) in enumerate(order):
        now = ahead
        if index + 1 < len(order):
            ahead = score(*order[index + 1])
        term = finish(block, other, *now)
        total = term if other == 0 else total + term
        if other == block:
            place = -(position + block * tile).astype(F32)
            slope_sum = slope_sum + jnp.where(
                mark < 2, total, jnp.where(mark == 5, total * place, 0.0)
            )
            keep(spans[block], cuts[0], total * 0.125)
    for rows in spans:
        keep(rows, cuts[1], key_sum[rows, :])
        keep(rows, cuts[2], value_sum[rows, :])
    return jnp.sum(jnp.where(here, 0.0, slope_sum))


def head_cuts(pair, width):
    return [
        pl.ds(pl.multiple_of(place * width + pair * LANES, LANES), LANES) for place in range(3)
    ]


def first_kernel(
    act_ref,
    cot_ref,
    ids_ref,
    gain_ref,
    slope_ref,
    proj_src,
    out_src,
    up_src,
    down_src,
    row_dst,
    proj_dst,
    out_dst,
    up_dst,
    down_dst,
    query_dst,
    keyval_dst,
    attended_dst,
    middle_dst,
    active_dst,
    slant_dst,
    grouped_dst,
    long_dst,
    pooled_dst,
    back_dst,
    small_all,
    key_mark,
    short_query_mark,
    short_key_mark,
    keep_ref,
    row_ref,
    proj_all,
    out_all,
    up_all,
    down_all,
    query_mark,
    wide_ref,
    mixed,
    queries,
    keys,
    values,
    attended,
    middle,
    actives,
    slants,
    moved,
    grouped,
    result,
    pooled_own,
    pooled,
    back,
    load_sem,
    row_send,
    row_recv,
    pair_send,
    pair_recv,
    pool_send,
    pool_recv,
    done_sem,
    *,
    tile,
    heads,
):
    section = lax.axis_index("section")
    group = lax.axis_index("dp")
    sections = 4
    core = section % 2
    chip = section // 2
    partner = chip * 2 + (1 - core)
    quarter, width = act_ref.shape[2:]
    length = row_ref.shape[0]
    short = length // 3
    groups = width // LANES
    units = up_all.shape[1]
    piece = units // PARTS
    blocks = length // tile

    def span_of(whole):
        rows = whole.shape[0] // 2
        return pl.ds(pl.multiple_of(core * rows, rows), rows)

    wholes = (proj_all, small_all, out_all, up_all, down_all)
    shards = (proj_src, None, out_src, up_src, down_src)

    def load_copy(index):
        return pltpu.make_async_copy(
            shards[index], wholes[index].at[span_of(wholes[index]), :], load_sem.at[index]
        )

    for index in (0, 2, 3, 4):
        load_copy(index).start()
    small_rows = span_of(small_all)
    small_all[small_rows, :] = jnp.concatenate(
        [
            gain_ref[...].astype(F32),
            jnp.concatenate(
                [
                    slope_ref[...].astype(F32),
                    jnp.zeros((1, width - slope_ref.shape[1]), F32),
                ],
                axis=1,
            ),
            jnp.zeros((6, width), F32),
        ],
        axis=0,
    )
    others = [lax.rem(section + hop, sections) for hop in range(1, sections)]
    barrier_with([(other, group) for other in others])
    place = pl.ds(pl.multiple_of(section * quarter, quarter), quarter)

    def row_copy(source_ref, hop):
        target = lax.rem(section + hop, sections)
        return pltpu.make_async_remote_copy(
            src_ref=source_ref.at[target % 2, 0],
            dst_ref=row_ref.at[place, :],
            send_sem=row_send.at[hop],
            recv_sem=row_recv.at[hop],
            device_id=(target, group),
            device_id_type=MESH,
        )

    for hop in (2, 1, 3):
        target_chip = lax.rem(section + hop, sections) // 2

        @pl.when(target_chip == 0)
        def _():
            row_copy(act_ref, hop).start()

        @pl.when(target_chip == 1)
        def _():
            row_copy(cot_ref, hop).start()

    def pair_copy(index):
        spot = wholes[index].at[span_of(wholes[index]), :]
        return pltpu.make_async_remote_copy(
            src_ref=spot,
            dst_ref=spot,
            send_sem=pair_send.at[index],
            recv_sem=pair_recv.at[index],
            device_id=(partner, group),
            device_id_type=MESH,
        )

    for index in range(len(wholes)):
        if shards[index] is not None:
            load_copy(index).wait()
        pair_copy(index).start()

    @pl.when(chip == 0)
    def _():
        row_ref[place, :] = act_ref[core, 0]

    @pl.when(chip == 1)
    def _():
        row_ref[place, :] = cot_ref[core, 0]

    ids = jnp.broadcast_to(ids_ref[core].astype(F32), (LANES, length))
    wide = ids.T
    wide_ref[0:8, :] = jnp.full((8, LANES), -1.0, F32)
    wide_ref[8:, :] = wide
    query_mark[...], key_mark[...] = make_marks(wide, lane_ids(length))
    short_wide = wide_ref[pl.ds(8, short, stride=3), :]
    short_query_mark[...], short_key_mark[...] = make_marks(short_wide, lane_ids(short))
    for turn in range(3):
        current = wide_ref[pl.ds(8 + turn, short, stride=3), :]
        before = wide_ref[pl.ds(6 + turn, short, stride=3), :]
        keep_ref[turn] = jnp.where(current == before, 1.0, 0.0)
    pair_copy(0).wait_recv()
    pair_copy(1).wait_recv()

    @pl.when(core == 0)
    def _():
        row_copy(act_ref, 3).wait_recv()

    @pl.when(core == 1)
    def _():
        row_copy(act_ref, 1).wait_recv()

    lane = lane_ids(tile)
    upper = lane >= HALF
    mark = lane % HALF
    sides = (jnp.logical_not(upper), upper)
    earlier = lax.broadcasted_iota(jnp.int32, (tile, tile), 0) >= lax.broadcasted_iota(
        jnp.int32, (tile, tile), 1
    )
    spans = [slice(block * tile, (block + 1) * tile) for block in range(blocks)]

    def project(rows):
        standard, _ = standardize(row_ref[rows, :].astype(F32))
        normal = (standard * small_all[0:1, :]).astype(BF16)
        mixed[rows, :] = dot(normal, proj_all[0:width, :], 1, 0).astype(BF16)

    def attend(members):
        def attend_pair(pair, carry):
            cuts = head_cuts(pair, width)
            column = lax.broadcasted_iota(jnp.int32, (1, width), 1)
            per = heads // 2
            slope_of = []
            for side in range(2):
                number = 2 * pair + side
                slopes = jnp.where(number < per, small_all[1:2, :], small_all[9:10, :])
                slope_of.append(
                    jnp.sum(
                        jnp.where(column == number % per, slopes, 0.0), axis=1, keepdims=True
                    )
                )
            for block in members:
                rows = spans[block]
                key_rows = mixed[rows, cuts[1]].astype(F32)
                value_rows = mixed[rows, cuts[2]].astype(F32)
                marks = key_mark[rows, :].astype(F32)
                for side, here in enumerate(sides):
                    keys[2 * pair + side, rows, :] = jnp.where(here, key_rows, marks).astype(BF16)
                    values[2 * pair + side, rows, :] = jnp.where(here, value_rows, 1.0).astype(
                        BF16
                    )

            def score(block, side):
                rows = spans[block]
                marks = jnp.where(mark < 2, slope_of[side], query_mark[rows, :].astype(F32))
                query = jnp.where(sides[side], mixed[rows, cuts[0]].astype(F32) * 0.125, marks)
                query = query.astype(BF16)
                number = 2 * pair + side
                near = jnp.where(earlier, dot(query, keys[number, rows, :], 1, 1), APART)
                far = dot(query, keys[number, : block * tile, :], 1, 1) if block else None
                return query, near, far

            def finish(block, side, query, near, far):
                rows = spans[block]
                number = 2 * pair + side
                highest = jnp.max(near, axis=1, keepdims=True)
                if block:
                    highest = jnp.maximum(highest, jnp.max(far, axis=1, keepdims=True))
                mass = dot(jnp.exp(near - highest).astype(BF16), values[number, rows, :], 1, 0)
                if block:
                    mass = mass + dot(
                        jnp.exp(far - highest).astype(BF16),
                        values[number, : block * tile, :],
                        1,
                        0,
                    )
                level = -(highest + jnp.log(mass))
                first = level.astype(BF16).astype(F32)
                second = (level - first).astype(BF16).astype(F32)
                third = level - first - second
                query = query.astype(F32)
                level_marks = jnp.where(
                    mark == 5,
                    first,
                    jnp.where(mark == 6, second, jnp.where(mark == 7, third, query)),
                )
                queries[number, rows, :] = jnp.where(sides[side], query, level_marks).astype(BF16)
                return mass / pltpu.roll(mass, HALF, 1)

            order = [(block, side) for block in members for side in range(2)]
            ahead = score(*order[0])
            shares = [None, None]
            for index, (block, side) in enumerate(order):
                now = ahead
                if index + 1 < len(order):
                    ahead = score(*order[index + 1])
                shares[side] = finish(block, side, *now)
                if side:
                    attended[spans[block], cuts[0]] = jnp.where(
                        upper, shares[1], shares[0]
                    ).astype(BF16)
            return carry

        lax.fori_loop(0, heads // 2, attend_pair, 0)

    def rows_wait_rest():
        row_copy(act_ref, 2).wait_recv()

        @pl.when(core == 0)
        def _():
            row_copy(act_ref, 1).wait_recv()

        @pl.when(core == 1)
        def _():
            row_copy(act_ref, 3).wait_recv()

    def pool_copy(block):
        rows = pl.ds(block * (tile // 3), tile // 3)
        return pltpu.make_async_remote_copy(
            src_ref=pooled_own.at[rows, :],
            dst_ref=pooled.at[rows, :],
            send_sem=pool_send.at[block],
            recv_sem=pool_recv.at[block],
            device_id=(lax.rem(section + 2, sections), group),
            device_id_type=MESH,
        )

    def out_copies(members=range(6)):
        kept = [
            (proj_all, proj_dst),
            (out_all, out_dst),
            (up_all, up_dst),
            (down_all, down_dst),
            (row_ref, row_dst),
            (grouped, grouped_dst),
        ]
        return [
            pltpu.make_async_copy(*kept[member], done_sem.at[member]) for member in members
        ]

    def attend_copies():
        kept = [
            (queries, query_dst),
            (mixed.at[:, pl.ds(width, 2 * width)], keyval_dst),
            (attended, attended_dst),
        ]
        return [
            pltpu.make_async_copy(origin, target, done_sem.at[6 + index])
            for index, (origin, target) in enumerate(kept)
        ]

    def tile_copies(block):
        rows = pl.ds(block * tile, tile)
        kept = [(middle, middle_dst), (actives, active_dst), (slants, slant_dst), (result, long_dst)]
        return [
            pltpu.make_async_copy(
                origin.at[rows, :], target.at[rows, :], done_sem.at[9 + 4 * block + index]
            )
            for index, (origin, target) in enumerate(kept)
        ]

    @pl.when(chip == 0)
    def _():
        for start in range(0, 2 * quarter, quarter):
            project(slice(start, start + quarter))
        attend((0,))

    rows_wait_rest()
    for index in range(2, len(wholes)):
        pair_copy(index).wait_recv()
    for copy in out_copies(range(5)):
        copy.start()

    @pl.when(chip == 0)
    def _():
        for start in range(2 * quarter, length, quarter):
            project(slice(start, start + quarter))
        attend(tuple(range(1, blocks)))
        for copy in attend_copies():
            copy.start()
        for part in range(groups):
            moved[part, 0:8, :] = jnp.zeros((8, LANES), F32)
        for block, rows in enumerate(spans):
            value = row_ref[rows, :].astype(F32) + dot(attended[rows, :], out_all[...], 1, 0)
            middle[rows, :] = value
            standard, _ = standardize(value)
            normal = (standard * small_all[8:9, :]).astype(BF16)
            for part in range(PARTS):
                span = slice(part * piece, (part + 1) * piece)
                active, slant = gelu_pieces(dot(normal, up_all[:, span], 1, 0))
                active = active.astype(BF16)
                actives[rows, span] = active
                slants[rows, span] = slant.astype(BF16)
                value = value + dot(active, down_all[span, :], 1, 0)
            low = value.astype(BF16)
            result[rows, :] = low
            for copy in tile_copies(block):
                copy.start()
            small_tile = tile // 3
            for part in range(groups):
                lanes = slice(part * LANES, (part + 1) * LANES)
                moved[part, 8 + block * tile : 8 + (block + 1) * tile, :] = low[:, lanes].astype(
                    F32
                )
            total = None
            small_rows = slice(block * small_tile, (block + 1) * small_tile)
            for turn in range(3):
                picked = jnp.concatenate(
                    [
                        moved[part, pl.ds(6 + turn + block * tile, small_tile, stride=3), :]
                        for part in range(groups)
                    ],
                    axis=1,
                )
                factor = jnp.concatenate([keep_ref[turn, small_rows, :]] * groups, axis=1)
                picked = (picked * factor).astype(BF16)
                cut = slice(turn * width, (turn + 1) * width)
                grouped[small_rows, cut] = picked
                term = dot(picked, proj_all[width : 2 * width, cut], 1, 1)
                total = term if total is None else total + term
            pooled_own[small_rows, :] = total.astype(BF16)
            pool_copy(block).start()

    @pl.when(chip == 1)
    def _():
        for part in range(groups):
            lanes = slice(part * LANES, (part + 1) * LANES)
            moved[part, 8:, :] = row_ref[:, lanes].astype(F32)
        for turn in range(3):
            for part in range(groups):
                left = turn * width + part * LANES
                grouped[:, left : left + LANES] = moved[
                    part, pl.ds(8 + turn, short, stride=3), :
                ].astype(BF16)
        back[...] = dot(grouped[...], proj_all[width : 2 * width, :], 1, 1).astype(BF16)
        back_copy = pltpu.make_async_copy(back, back_dst, done_sem.at[21])
        back_copy.start()
        long_copy = pltpu.make_async_copy(row_ref, long_dst, done_sem.at[22])
        long_copy.start()
        back_copy.wait()
        long_copy.wait()
        for block in range(blocks):
            pool_copy(block).wait_recv()
        pooled_copy = pltpu.make_async_copy(pooled, pooled_dst, done_sem.at[23])
        pooled_copy.start()
        pooled_copy.wait()

    out_copies([5])[0].start()

    @pl.when(chip == 0)
    def _():
        for copy in attend_copies():
            copy.wait()
        for block in range(blocks):
            for copy in tile_copies(block):
                copy.wait()
            pool_copy(block).wait_send()

    for copy in out_copies():
        copy.wait()
    for index in range(len(wholes)):
        pair_copy(index).wait_send()
    for hop in range(1, sections):
        row_copy(act_ref, hop).wait_send()


def first_call(
    activations, cotangent, ids, gains, slopes, proj, out_rows, up_rows, down_rows, heads, tile
):
    inside = pl.BlockSpec(memory_space=pltpu.VMEM)
    anywhere = pl.BlockSpec(memory_space=pl.ANY)
    quarter, width = activations.shape[2:]
    length = 4 * quarter
    short = length // 3
    units = up_rows.shape[1]
    shape = jax.ShapeDtypeStruct
    vmem = pltpu.VMEM
    twice = lambda value: (2 * value.shape[0], value.shape[1])
    weights = [twice(value) for value in (proj, out_rows, up_rows, down_rows)]
    return pl.pallas_call(
        functools.partial(first_kernel, tile=tile, heads=heads),
        in_specs=[inside] * 5 + [anywhere] * 4,
        out_specs=[anywhere] * 15 + [inside] * 5,
        out_shape=[shape((length, width), BF16)]
        + [shape(size, BF16) for size in weights]
        + [
            shape((heads, length, LANES), BF16),
            shape((length, 2 * width), BF16),
            shape((length, width), BF16),
            shape((length, width), F32),
            shape((length, units), BF16),
            shape((length, units), BF16),
            shape((short, 3 * width), BF16),
            shape((length, width), BF16),
            shape((short, width), BF16),
            shape((short, width), BF16),
            shape((16, width), F32),
            shape((length, LANES), BF16),
            shape((short, LANES), BF16),
            shape((short, LANES), BF16),
            shape((3, short, LANES), F32),
        ],
        scratch_shapes=[vmem((length, width), BF16)]
        + [vmem(size, BF16) for size in weights]
        + [
            vmem((length, LANES), BF16),
            vmem((length + 8, LANES), F32),
            vmem((length, 3 * width), BF16),
            vmem((heads, length, LANES), BF16),
            vmem((heads, length, LANES), BF16),
            vmem((heads, length, LANES), BF16),
            vmem((length, width), BF16),
            vmem((length, width), F32),
            vmem((length, units), BF16),
            vmem((length, units), BF16),
            vmem((width // LANES, length + 8, LANES), F32),
            vmem((short, 3 * width), BF16),
            vmem((length, width), BF16),
            vmem((short, width), BF16),
            vmem((short, width), BF16),
            vmem((short, width), BF16),
            pltpu.SemaphoreType.DMA((5,)),
            pltpu.SemaphoreType.DMA((4,)),
            pltpu.SemaphoreType.DMA((4,)),
            pltpu.SemaphoreType.DMA((5,)),
            pltpu.SemaphoreType.DMA((5,)),
            pltpu.SemaphoreType.DMA((3,)),
            pltpu.SemaphoreType.DMA((3,)),
            pltpu.SemaphoreType.DMA((24,)),
        ],
        compiler_params=pltpu.CompilerParams(
            collective_id=0, has_side_effects=True, vmem_limit_bytes=VMEM_LIMIT
        ),
        name="first",
    )(activations, cotangent, ids, gains, slopes, proj, out_rows, up_rows, down_rows)


def short_kernel(
    hidden_ref,
    grad_ref,
    gain_ref,
    query_mark_ref,
    key_mark_ref,
    proj_src,
    out_src,
    up_src,
    down_src,
    result_dst,
    hidden_dst,
    even_dst,
    out_dst,
    up_dst,
    down_dst,
    small_ref,
    proj_ref,
    out_ref,
    up_ref,
    down_ref,
    result_ref,
    hidden_grad,
    even_grad,
    out_grad,
    up_grad,
    down_grad,
    mixed,
    queries,
    keys,
    values,
    grads,
    key_sum,
    value_sum,
    attended,
    middle,
    total,
    normal,
    flip,
    grad_flip,
    actives,
    slants,
    attended_grad,
    mixed_grad,
    load_sem,
    done_sem,
    *,
    heads,
):
    length, width = hidden_ref.shape
    units = up_ref.shape[1]
    piece = units // PARTS
    loads = [
        pltpu.make_async_copy(origin, target, load_sem.at[index])
        for index, (origin, target) in enumerate(
            (
                (proj_src.at[0:width, :], proj_ref),
                (out_src, out_ref),
                (up_src, up_ref),
                (down_src, down_ref),
            )
        )
    ]
    for copy in loads:
        copy.start()
    lane = lane_ids(length)
    upper = lane >= HALF
    mark = lane % HALF
    earlier = lax.broadcasted_iota(jnp.int32, (length, length), 0) >= lax.broadcasted_iota(
        jnp.int32, (length, length), 1
    )
    standard, _ = standardize(hidden_ref[...].astype(F32))
    low = (standard * gain_ref[0:1, :]).astype(BF16)
    flip[...] = low.T
    loads[0].wait()
    mixed[...] = dot(low, proj_ref[...], 1, 0).astype(BF16)
    small_ref[...] = jnp.zeros_like(small_ref)
    column = lax.broadcasted_iota(jnp.int32, (1, width), 1)
    sides = (jnp.logical_not(upper), upper)
    per = heads // 2

    def attend_pair(pair, carry):
        cuts = head_cuts(pair, width)
        query_rows = mixed[:, cuts[0]].astype(F32) * 0.125
        key_rows = mixed[:, cuts[1]].astype(F32)
        value_rows = mixed[:, cuts[2]].astype(F32)
        scores, parts = [], []
        for side, here in enumerate(sides):
            number = 2 * pair + side
            slopes = jnp.where(number < per, gain_ref[1:2, :], gain_ref[9:10, :])
            slope = jnp.sum(jnp.where(column == number % per, slopes, 0.0), axis=1, keepdims=True)
            keys[side] = jnp.where(here, key_rows, key_mark_ref[...].astype(F32)).astype(BF16)
            values[side] = jnp.where(here, value_rows, 1.0).astype(BF16)
            marks = jnp.where(mark < 2, slope, query_mark_ref[...].astype(F32))
            query = jnp.where(here, query_rows, marks).astype(BF16)
            parts.append(query)
            scores.append(jnp.where(earlier, dot(query, keys[side], 1, 1), APART))
        shares = []
        for side, here in enumerate(sides):
            highest = jnp.max(scores[side], axis=1, keepdims=True)
            mass = dot(jnp.exp(scores[side] - highest).astype(BF16), values[side], 1, 0)
            level = -(highest + jnp.log(mass))
            first = level.astype(BF16).astype(F32)
            second = (level - first).astype(BF16).astype(F32)
            third = level - first - second
            query = parts[side].astype(F32)
            level_marks = jnp.where(
                mark == 5, first, jnp.where(mark == 6, second, jnp.where(mark == 7, third, query))
            )
            queries[2 * pair + side] = jnp.where(here, query, level_marks).astype(BF16)
            shares.append(mass / pltpu.roll(mass, HALF, 1))
        attended[:, cuts[0]] = jnp.where(upper, shares[1], shares[0]).astype(BF16)
        return carry

    lax.fori_loop(0, heads // 2, attend_pair, 0)
    loads[1].wait()
    value = hidden_ref[...].astype(F32) + dot(attended[...], out_ref[...], 1, 0)
    middle[...] = value
    total[...] = value
    standard, _ = standardize(value)
    normal[...] = (standard * gain_ref[8:9, :]).astype(BF16)
    loads[2].wait()
    loads[3].wait()
    for part in range(PARTS):
        span = slice(part * piece, (part + 1) * piece)
        raised = dot(normal[...], up_ref[:, span], 1, 0)
        active, slant = gelu_pieces(raised)
        active = active.astype(BF16)
        actives[:, span] = active
        slants[:, span] = slant.astype(BF16)
        total[...] += dot(active, down_ref[span, :], 1, 0)
    result_ref[...] = total[...].astype(BF16)
    results = [pltpu.make_async_copy(result_ref, result_dst, done_sem.at[0])]
    results[0].start()

    grad_flip[...] = grad_ref[...].T
    normal_flip = normal[...].T
    for part in range(PARTS):
        span = slice(part * piece, (part + 1) * piece)
        down_grad[span, :] = dot(grad_flip[...], actives[:, span], 1, 0).astype(BF16).T
        grad_active = dot(grad_ref[...], down_ref[span, :], 1, 1)
        low = (grad_active * slants[:, span].astype(F32)).astype(BF16)
        term = dot(low, up_ref[:, span], 1, 1)
        if part:
            total[...] += term
        else:
            total[...] = term
        up_grad[:, span] = dot(normal_flip, low, 1, 0).astype(BF16)
    for index, (origin, target) in enumerate(((down_grad, down_dst), (up_grad, up_dst))):
        results.append(pltpu.make_async_copy(origin, target, done_sem.at[1 + index]))
        results[-1].start()
    standard, inverse = standardize(middle[...])
    grad = total[...]
    small_ref[1:2, :] = jnp.sum(grad * standard, axis=0, keepdims=True)
    middle_grad = grad_ref[...].astype(F32) + norm_back(grad, gain_ref[8:9, :], standard, inverse)
    total[...] = middle_grad
    low = middle_grad.astype(BF16)
    attended_grad[...] = dot(low, out_ref[...], 1, 1).astype(BF16)
    out_grad[...] = dot(attended[...], low, 0, 0).astype(BF16)
    results.append(pltpu.make_async_copy(out_grad, out_dst, done_sem.at[3]))
    results[-1].start()

    def back_pair(pair, carry):
        cuts = head_cuts(pair, width)
        for side in range(2):
            slope_grad = head_back(
                side, key_mark_ref, queries.at[pl.ds(2 * pair + side, 1)], mixed.at[:, cuts[1]],
                mixed.at[:, cuts[2]], attended.at[:, cuts[0]], attended_grad.at[:, cuts[0]],
                mixed_grad, keys.at[side], values.at[side], grads.at[side], key_sum.at[side],
                value_sum.at[side], cuts, length,
            )
            small_ref[2:3, :] += jnp.where(column == 2 * pair + side, slope_grad, 0.0)
        return carry

    lax.fori_loop(0, heads // 2, back_pair, 0)
    for place in range(3):
        span = slice(place * width, (place + 1) * width)
        even_grad[:, span] = dot(flip[...], mixed_grad[:, span], 1, 0).astype(BF16)
    results.append(pltpu.make_async_copy(even_grad, even_dst, done_sem.at[4]))
    results[-1].start()
    standard, inverse = standardize(hidden_ref[...].astype(F32))
    grad = dot(mixed_grad[...], proj_ref[...], 1, 1)
    small_ref[0:1, :] = jnp.sum(grad * standard, axis=0, keepdims=True)
    hidden_grad[...] = (
        total[...] + norm_back(grad, gain_ref[0:1, :], standard, inverse)
    ).astype(BF16)
    results.append(pltpu.make_async_copy(hidden_grad, hidden_dst, done_sem.at[5]))
    results[-1].start()
    for copy in results:
        copy.wait()


def short_call(
    hidden, grad, gains, query_mark, key_mark, proj, out_weight, up_weight, down_weight, heads
):
    inside = pl.BlockSpec(memory_space=pltpu.VMEM)
    anywhere = pl.BlockSpec(memory_space=pl.ANY)
    length, width = hidden.shape
    units = up_weight.shape[1]
    vmem = pltpu.VMEM
    shape = jax.ShapeDtypeStruct
    grads = [(width, 3 * width), out_weight.shape, up_weight.shape, down_weight.shape]
    return pl.pallas_call(
        functools.partial(short_kernel, heads=heads),
        in_specs=[inside] * 5 + [anywhere] * 4,
        out_specs=[anywhere] * 6 + [inside],
        out_shape=[shape((length, width), BF16)] * 2
        + [shape(size, BF16) for size in grads]
        + [shape((8, width), F32)],
        scratch_shapes=[
            vmem((width, 3 * width), BF16),
            vmem(out_weight.shape, BF16),
            vmem(up_weight.shape, BF16),
            vmem(down_weight.shape, BF16),
            vmem((length, width), BF16),
            vmem((length, width), BF16),
        ]
        + [vmem(size, BF16) for size in grads]
        + [
            vmem((length, 3 * width), BF16),
            vmem((heads, length, LANES), BF16),
            vmem((2, length, LANES), BF16),
            vmem((2, length, LANES), BF16),
            vmem((2, length, LANES), BF16),
            vmem((2, length, LANES), F32),
            vmem((2, length, LANES), F32),
            vmem((length, width), BF16),
            vmem((length, width), F32),
            vmem((length, width), F32),
            vmem((length, width), BF16),
            vmem((width, length), BF16),
            vmem((width, length), BF16),
            vmem((length, units), BF16),
            vmem((length, units), BF16),
            vmem((length, width), BF16),
            vmem((length, 3 * width), BF16),
            pltpu.SemaphoreType.DMA((4,)),
            pltpu.SemaphoreType.DMA((6,)),
        ],
        compiler_params=params(),
        name="short",
    )(hidden, grad, gains, query_mark, key_mark, proj, out_weight, up_weight, down_weight)


def chunk_list():
    chunks = [("odd", 1, 0, 512, place * 512, 512) for place in range(3)]
    chunks += [("up", None, 0, 256, place * 512, 512) for place in (0, 2)]
    chunks += [("down", None, 0, 512, 0, 512)]
    chunks += [("up", None, 0, 256, place * 512, 512) for place in (1, 3)]
    chunks += [("down", None, 512, 512, 0, 512)]
    chunks += [("out", None, 0, 256, 0, 512)]
    chunks += [("even", 0, 0, 512, pair * 384, 384) for pair in range(4)]
    return chunks


BEGINS = {1: (3,), 2: (4, 5), 3: (6,), 4: (7, 8, 9), 6: (10,), 8: (11,), 10: (12,), 12: (13,)}
TICKS = {
    3: [
        ("pair", 3), ("side", 1), ("side", 2), ("line", 0),
    ],
    4: [
        ("pair", 5), ("side", 3), ("line", 1), ("line", 2), ("side", 4),
    ],
    5: [
        ("line", 3), ("side", 5),
    ],
    6: [
        ("back", 1), ("side", 6), ("pair", 7), ("pair", 9), ("back", 2), ("pair", 8),
        ("full", 0), ("line", 4),
    ],
    7: [
        ("full", 1), ("back", 3), ("side", 7),
    ],
    8: [
        ("pair", 10), ("side", 9), ("line", 5), ("full", 2), ("line", 6),
    ],
    9: [
        ("back", 4), ("side", 8),
    ],
    10: [
        ("line", 7), ("pair", 11), ("full", 3), ("line", 9), ("side", 10),
    ],
    11: [
        ("full", 4), ("back", 5), ("side", 11),
    ],
    12: [
        ("back", 6), ("pair", 12),
    ],
    13: [
        ("line", 8), ("full", 5),
    ],
}
MIDDLES = {
    1: [
        ("pair", 0), ("pair", 1), ("pair", 2),
    ],
    2: [
        ("side", 0),
    ],
    3: [
        ("pair", 4),
    ],
    4: [
        ("pair", 6), ("back", 0),
    ],
}
DRAIN = [
    ("full", 6), ("back", 7), ("pair", 13), ("side", 12), ("back", 9), ("line", 10),
    ("line", 11), ("full", 7), ("side", 13), ("back", 8), ("full", 9), ("line", 12),
    ("back", 10), ("back", 11), ("full", 8), ("line", 13), ("full", 10), ("back", 12),
    ("full", 11), ("back", 13), ("full", 12), ("full", 13),
]


def last_kernel(
    hidden_src,
    gain_ref,
    proj_ref,
    key_mark_src,
    middle_src,
    attended_src,
    out_weight_src,
    keep_ref,
    grouped_ref,
    added_ref,
    active_ref,
    slant_ref,
    up_weight_ref,
    down_weight_ref,
    query_ref,
    key_ref,
    value_ref,
    pooled_grad_ref,
    short_result_ref,
    even_ref,
    out_ref,
    up_ref,
    down_ref,
    small_ref,
    proj_result,
    out_result,
    up_result,
    down_result,
    small_result,
    parts_result,
    middle_ref,
    attended_ref,
    out_weight_ref,
    hidden_ref,
    key_mark_ref,
    short_rows,
    sent_rows,
    moved,
    rows_buf,
    normal,
    grad_flip,
    total,
    lower,
    attended_grad,
    mixed,
    keys,
    values,
    grads,
    key_sum,
    value_sum,
    even_grad,
    odd_grad,
    out_grad,
    up_grad,
    down_grad,
    small_grad,
    small_full,
    parts_ref,
    proj_full,
    out_full,
    up_full,
    down_full,
    proj_pair,
    out_pair,
    up_pair,
    down_pair,
    proj_side,
    out_side,
    up_side,
    down_side,
    proj_line,
    out_line,
    up_line,
    down_line,
    small_pair,
    small_side,
    small_line,
    local_sem,
    pair_send,
    pair_recv,
    side_send,
    side_recv,
    line_send,
    line_recv,
    back_send,
    back_recv,
    full_send,
    full_recv,
    small_send,
    small_recv,
    rows_send,
    rows_recv,
    result_sem,
    load_sem,
    short_send,
    short_recv,
    *,
    tile,
):
    step = pl.program_id(0)
    last = pl.num_programs(0) - 1
    section = lax.axis_index("section")
    group = lax.axis_index("dp")
    core = section % 2
    chip = section // 2
    partner = (chip * 2 + (1 - core), group)
    base = group // SQUARE * SQUARE
    side = group % 2
    line = group % SQUARE // 2
    neighbour = (section, base + line * 2 + (1 - side))
    length, width = hidden_ref.shape
    short = length // 3
    groups = width // LANES
    stride = min(length // 2, 384)
    quarter = parts_ref.shape[1]
    chunks = chunk_list()
    first_head = 1 + PARTS

    def along(hop):
        return (section, base + lax.rem(line + hop, LINE) * 2 + side)

    def across(hop):
        return lax.rem(section + hop, 4)

    source = {"odd": odd_grad, "even": even_grad, "out": out_grad, "up": up_grad, "down": down_grad}
    table = lambda proj, out, up, down: {
        "odd": proj, "even": proj, "out": out, "up": up, "down": down
    }
    sums = table(proj_pair, out_pair, up_pair, down_pair)
    sides = table(proj_side, out_side, up_side, down_side)
    lines = table(proj_line, out_line, up_line, down_line)
    fulls = table(proj_full, out_full, up_full, down_full)
    outcomes = table(proj_result, out_result, up_result, down_result)

    def cut(start, size):
        return pl.ds(pl.multiple_of(start, 16), size)

    def remote(origin, target, send, recv, device):
        return pltpu.make_async_remote_copy(
            src_ref=origin,
            dst_ref=target,
            send_sem=send,
            recv_sem=recv,
            device_id=device,
            device_id_type=MESH,
        )

    def pair_copy(index):
        name, owner, start, rows, left, cols = chunks[index]
        offset = 0 if owner is not None else (1 - core) * (source[name].shape[0] // 2)
        lanes = pl.ds(left, cols)
        return remote(
            source[name].at[cut(offset + start, rows), lanes],
            sums[name].at[cut(start, rows), lanes],
            pair_send.at[index],
            pair_recv.at[index],
            partner,
        )

    def side_copy(index):
        name, _, start, rows, left, cols = chunks[index]
        half = rows // 2
        lanes = pl.ds(left, cols)
        return remote(
            sums[name].at[cut(start + (1 - side) * half, half), lanes],
            sides[name].at[cut(start // 2, half), lanes],
            side_send.at[index],
            side_recv.at[index],
            neighbour,
        )

    def line_copy(index, hop):
        name, _, start, rows, left, cols = chunks[index]
        half, piece = rows // 2, rows // SQUARE
        lanes = pl.ds(left, cols)
        target = lax.rem(line + hop, LINE)
        return remote(
            sums[name].at[cut(start + side * half + target * piece, piece), lanes],
            lines[name].at[hop - 1, cut(start // SQUARE, piece), lanes],
            line_send.at[index, hop - 1],
            line_recv.at[index, hop - 1],
            along(hop),
        )

    def back_copy(index, hop):
        name, _, start, rows, left, cols = chunks[index]
        half, piece = rows // 2, rows // SQUARE
        place = fulls[name].at[
            cut(start + side * half + line * piece, piece), pl.ds(left, cols)
        ]
        return remote(
            place, place, back_send.at[index, hop - 1], back_recv.at[index, hop - 1], along(hop)
        )

    def full_copy(index):
        name, _, start, rows, left, cols = chunks[index]
        half = rows // 2
        place = fulls[name].at[cut(start + side * half, half), pl.ds(left, cols)]
        return remote(place, place, full_send.at[index], full_recv.at[index], neighbour)

    def result_copies(index):
        name, _, start, rows, left, cols = chunks[index]
        spans = [(pl.ds(left, cols), pl.ds(left, cols))]
        if name == "even":
            spans = [span for span in regroup() if left <= span[1].start < left + cols]
        return [
            pltpu.make_async_copy(
                fulls[name].at[cut(start, rows), held],
                outcomes[name].at[cut(start, rows), final],
                result_sem.at[index, number],
            )
            for number, (final, held) in enumerate(spans)
        ]

    def owned(index, act):
        owner = chunks[index][1]
        if owner is None:
            act()
        else:
            pl.when(core == owner)(act)

    def pair_start(index):
        owner = chunks[index][1]
        begin = lambda: pair_copy(index).start()
        if owner is None:
            begin()
        else:
            pl.when(core != owner)(begin)

    def pair_stage(index):
        name, owner, start, rows, left, cols = chunks[index]
        lanes = slice(left, left + cols)
        here = cut(start, rows)

        def act():
            pair_copy(index).wait_recv()
            offset = 0 if owner is not None else core * (source[name].shape[0] // 2)
            mine = source[name][cut(offset + start, rows), lanes].astype(F32)
            arrived = sums[name][here, lanes].astype(F32)
            sums[name][here, lanes] = (mine + arrived).astype(BF16)
            side_copy(index).start()

        if owner is None:
            pair_copy(index).wait_send()
        else:
            pl.when(core != owner)(lambda: pair_copy(index).wait_send())
        owned(index, act)

    def side_stage(index):
        name, _, start, rows, left, cols = chunks[index]
        half = rows // 2
        lanes = slice(left, left + cols)

        def act():
            side_copy(index).wait()
            here = cut(start + side * half, half)
            arrived = sides[name][cut(start // 2, half), lanes].astype(F32)
            sums[name][here, lanes] = (sums[name][here, lanes].astype(F32) + arrived).astype(BF16)
            for hop in range(1, LINE):
                line_copy(index, hop).start()

        owned(index, act)

    def line_stage(index):
        name, _, start, rows, left, cols = chunks[index]
        half, piece = rows // 2, rows // SQUARE
        lanes = slice(left, left + cols)

        def act():
            for hop in range(1, LINE):
                line_copy(index, hop).wait()
            here = cut(start + side * half + line * piece, piece)
            value = sums[name][here, lanes].astype(F32)
            for hop in range(1, LINE):
                value = value + lines[name][hop - 1, cut(start // SQUARE, piece), lanes].astype(F32)
            fulls[name][here, lanes] = value.astype(BF16)
            for hop in range(1, LINE):
                back_copy(index, hop).start()

        owned(index, act)

    def back_stage(index):
        def act():
            for hop in range(1, LINE):
                back_copy(index, hop).wait()
            full_copy(index).start()

        owned(index, act)

    def full_stage(index):
        def act():
            full_copy(index).wait()
            for copy in result_copies(index):
                copy.start()

        owned(index, act)

    def result_wait(index):
        for copy in result_copies(index):
            copy.wait()

    stages = {
        "pair": pair_stage,
        "side": side_stage,
        "line": line_stage,
        "back": back_stage,
        "full": full_stage,
    }

    def rows_copy(hop):
        target = across(hop)
        return remote(
            rows_buf.at[cut(target * quarter, quarter), :],
            parts_ref.at[section],
            rows_send.at[hop],
            rows_recv.at[hop],
            (target, group),
        )

    def load_copies():
        pairs = [
            (out_ref, out_grad),
            (up_ref, up_grad),
            (down_ref, down_grad),
            (small_ref, small_grad),
        ]
        pairs += [
            (even_ref.at[:, origin], even_grad.at[:, target]) for origin, target in regroup()
        ]
        return [
            pltpu.make_async_copy(origin, target, load_sem.at[index])
            for index, (origin, target) in enumerate(pairs)
        ]

    def regroup():
        for pair in range(width // LANES):
            for place in range(3):
                yield (
                    pl.ds(place * width + pair * LANES, LANES),
                    pl.ds((3 * pair + place) * LANES, LANES),
                )

    def kept_copies(members=range(5)):
        pairs = (
            (middle_src, middle_ref),
            (attended_src, attended_ref),
            (out_weight_src, out_weight_ref),
            (hidden_src, hidden_ref),
            (key_mark_src, key_mark_ref),
        )
        return [
            pltpu.make_async_copy(*pairs[member], local_sem.at[1 + member]) for member in members
        ]

    def kept_wait(*members):
        for copy in kept_copies(members):
            copy.wait()

    @pl.when(step == 0)
    def _():
        @pl.when(chip == 0)
        def _():
            for copy in kept_copies():
                copy.start()
            small_grad[...] = jnp.zeros_like(small_grad)

        @pl.when(chip == 1)
        def _():
            pltpu.make_async_copy(pooled_grad_ref, sent_rows, local_sem.at[0]).start()
            pltpu.make_async_copy(short_result_ref, short_rows, local_sem.at[6]).start()
            for copy in load_copies():
                copy.start()

        barrier_with(
            [(across(hop), group) for hop in range(1, 4)]
            + [neighbour]
            + [along(hop) for hop in range(1, LINE)]
        )
        short_copy = remote(
            sent_rows, short_rows, short_send.at[0], short_recv.at[0], (across(2), group)
        )

        @pl.when(chip == 0)
        def _():
            short_copy.wait_recv()

        @pl.when(chip == 1)
        def _():
            pltpu.make_async_copy(pooled_grad_ref, sent_rows, local_sem.at[0]).wait()
            short_copy.start()
            pltpu.make_async_copy(short_result_ref, short_rows, local_sem.at[6]).wait()

        rows = short_rows[...]
        flip = rows.T
        for place in range(3):
            lanes = slice(place * width, (place + 1) * width)
            odd_grad[:, lanes] = dot(flip, grouped_ref[:, lanes], 1, 0).astype(BF16)
            pair_start(place)
        for place in range(3):
            lanes = slice(place * width, (place + 1) * width)
            spread_rows = dot(rows, proj_ref[width : 2 * width, lanes], 1, 0)
            factor = jnp.maximum(keep_ref[place], chip.astype(F32))
            for part in range(groups):
                moved[part, pl.ds(place, short, stride=3), :] = (
                    spread_rows[:, part * LANES : (part + 1) * LANES] * factor
                )
        for part in range(groups):
            lanes = slice(part * LANES, (part + 1) * LANES)
            moved[part, length:, :] = jnp.zeros((8, LANES), F32)
            added = added_ref[:, lanes].astype(F32)

            @pl.when(chip == 0)
            def _():
                rows_buf[:, lanes] = (added + moved[part, 2 : 2 + length, :]).astype(BF16)

            @pl.when(chip == 1)
            def _():
                rows_buf[:, lanes] = (added + moved[part, 0:length, :]).astype(BF16)

        @pl.when(chip == 1)
        def _():
            for copy in load_copies():
                copy.wait()
            short_copy.wait_send()

    for tick, events in TICKS.items():

        @pl.when(step == tick)
        def _():
            for stage, index in events:
                stages[stage](index)

    @pl.when((chip == 0) & (step == 1))
    def _():
        kept_wait(0)
        for rows in row_cuts(length, stride):
            standard, _ = standardize(middle_ref[rows, :])
            normal[:, rows] = (standard * gain_ref[8:9, :]).astype(BF16).T
            grad_flip[:, rows] = rows_buf[rows, :].T
            total[rows, :] = jnp.zeros((stride, width), F32)

    @pl.when((chip == 0) & (step >= 1) & (step < first_head))
    def _():
        turn = step - 1
        part = (turn % 2) * 2 + turn // 2
        span = pl.ds(pl.multiple_of(part * 512, 512), 512)
        down_grad[span, :] = dot(grad_flip[...], active_ref[...], 1, 0).astype(BF16).T

    for tick, events in MIDDLES.items():

        @pl.when(step == tick)
        def _():
            for stage, index in events:
                stages[stage](index)

    @pl.when((chip == 0) & (step >= 1) & (step < first_head))
    def _():
        turn = step - 1
        part = (turn % 2) * 2 + turn // 2
        span = pl.ds(pl.multiple_of(part * 512, 512), 512)
        for rows in row_cuts(length, stride):
            grad_active = dot(rows_buf[rows, :], down_weight_ref[...], 1, 1)
            low = (grad_active * slant_ref[rows, :].astype(F32)).astype(BF16)
            lower[rows, :] = low
            total[rows, :] += dot(low, up_weight_ref[...], 1, 1)
        up_grad[:, span] = dot(normal[...], lower[...], 1, 0).astype(BF16)

    @pl.when((chip == 0) & (step == first_head - 1))
    def _():
        kept_wait(1, 2)
        gain_sum = jnp.zeros((1, width), F32)
        for rows in row_cuts(length, stride):
            standard, inverse = standardize(middle_ref[rows, :])
            grad = total[rows, :]
            gain_sum = gain_sum + jnp.sum(grad * standard, axis=0, keepdims=True)
            middle_grad = rows_buf[rows, :].astype(F32) + norm_back(
                grad, gain_ref[8:9, :], standard, inverse
            )
            total[rows, :] = middle_grad
            low = middle_grad.astype(BF16)
            lower[rows, :] = low
            attended_grad[rows, :] = dot(low, out_weight_ref[...], 1, 1).astype(BF16)
        small_grad[1:2, :] = gain_sum
        out_grad[...] = dot(attended_ref[...], lower[...], 0, 0).astype(BF16)

    @pl.when((chip == 0) & (step == first_head))
    def _():
        kept_wait(3, 4)
        for rows in row_cuts(length, stride):
            standard, _ = standardize(hidden_ref[rows, :].astype(F32))
            normal[:, rows] = (standard * gain_ref[0:1, :]).astype(BF16).T

    @pl.when((chip == 0) & (step >= first_head) & (step < last))
    def _():
        head = step - first_head
        cuts = head_cuts(head // 2, width)
        slope_grad = head_back(
            head % 2, key_mark_ref, query_ref, key_ref, value_ref, attended_ref.at[:, cuts[0]],
            attended_grad.at[:, cuts[0]], mixed, keys, values, grads, key_sum, value_sum,
            cuts, tile,
        )
        column = lax.broadcasted_iota(jnp.int32, (1, width), 1)
        small_grad[2:3, :] += jnp.where(column == head, slope_grad, 0.0)

    @pl.when((chip == 0) & (step >= first_head) & (step < last) & (step % 2 == 0))
    def _():
        pair = (step - first_head) // 2
        for place, span in enumerate(head_cuts(pair, width)):
            target = pl.ds(pl.multiple_of((3 * pair + place) * LANES, LANES), LANES)
            even_grad[:, target] = dot(normal[...], mixed[:, span], 1, 0).astype(BF16)

    for begin, members in BEGINS.items():
        @pl.when(step == begin)
        def _():
            for index in members:
                pair_start(index)

    @pl.when((chip == 0) & (step == last))
    def _():
        gain_sum = jnp.zeros((1, width), F32)
        for rows in row_cuts(length, stride):
            standard, inverse = standardize(hidden_ref[rows, :].astype(F32))
            grad = dot(mixed[rows, :], proj_ref[0:width, :], 1, 1)
            gain_sum = gain_sum + jnp.sum(grad * standard, axis=0, keepdims=True)
            rows_buf[rows, :] = (
                total[rows, :] + norm_back(grad, gain_ref[0:1, :], standard, inverse)
            ).astype(BF16)
        small_grad[0:1, :] = gain_sum

    @pl.when(step == last)
    def _():
        small_one = remote(small_grad, small_pair, small_send.at[0], small_recv.at[0], partner)
        small_one.start()
        for hop in range(1, 4):
            rows_copy(hop).start()
        parts_ref[section] = rows_buf[cut(section * quarter, quarter), :]
        for stage, index in DRAIN[:3]:
            stages[stage](index)
        small_one.wait()
        small_full[...] = small_grad[...] + small_pair[...]
        small_two = remote(small_full, small_side, small_send.at[1], small_recv.at[1], neighbour)
        small_two.start()
        for stage, index in DRAIN[3:7]:
            stages[stage](index)
        small_two.wait()
        small_full[...] = small_full[...] + small_side[...]
        small_rest = [
            remote(
                small_full,
                small_line.at[line],
                small_send.at[1 + hop],
                small_recv.at[1 + hop],
                along(hop),
            )
            for hop in range(1, LINE)
        ]
        for copy in small_rest:
            copy.start()
        for stage, index in DRAIN[7:]:
            stages[stage](index)
        for copy in small_rest:
            copy.wait()
        small_line[line] = small_full[...]
        small_result[...] = (small_line[0] + small_line[1]) + (small_line[2] + small_line[3])
        for hop in range(1, 4):
            rows_copy(hop).wait()
        parts_copy = pltpu.make_async_copy(parts_ref, parts_result, result_sem.at[len(chunks), 0])
        parts_copy.start()
        for index in range(len(chunks)):
            owned(index, functools.partial(result_wait, index))
        parts_copy.wait()


def last_call(
    hidden, gains, proj, key_mark, middle, attended, out_weight, keep, grouped, added,
    active, slant, up_weight, down_weight, query, keyval,
    pooled_grad, short_result, even, out_grad, up_grad, down_grad, small, tile,
):
    inside = pl.BlockSpec(memory_space=pltpu.VMEM)
    anywhere = pl.BlockSpec(memory_space=pl.ANY)
    length, width = hidden.shape
    short = length // 3
    heads = query.shape[0]
    units = up_weight.shape[1]
    wide = even.shape[1]
    piece = units // PARTS
    half = lambda value: (value.shape[0] // 2, value.shape[1])
    shapes = [even.shape, half(out_grad), half(up_grad), half(down_grad)]
    count = len(chunk_list())
    vmem = pltpu.VMEM
    scaled = lambda over: [vmem((rows // over, cols), BF16) for rows, cols in shapes]
    semaphores = lambda *shape: [pltpu.SemaphoreType.DMA(shape)] * 2

    def part_of(step):
        turn = jnp.clip(step - 1, 0, PARTS - 1)
        return turn % 2 * 2 + turn // 2

    def head_of(step):
        return jnp.clip(step - 1 - PARTS, 0, heads - 1)

    column = lambda start: pl.BlockSpec(
        (length, LANES), lambda step: (0, start + head_of(step) // 2)
    )
    results = pl.pallas_call(
        functools.partial(last_kernel, tile=tile),
        grid=(2 + PARTS + heads,),
        in_specs=[anywhere, inside, inside] + [anywhere] * 4 + [inside] * 3
        + [pl.BlockSpec((length, piece), lambda step: (0, part_of(step)))] * 2
        + [
            pl.BlockSpec((width, piece), lambda step: (0, part_of(step))),
            pl.BlockSpec((piece, width), lambda step: (part_of(step), 0)),
            pl.BlockSpec((1, length, LANES), lambda step: (head_of(step), 0, 0)),
            column(0),
            column(heads // 2),
        ]
        + [anywhere] * 7,
        out_specs=[anywhere] * 4 + [inside, anywhere],
        out_shape=[jax.ShapeDtypeStruct(shape, BF16) for shape in shapes]
        + [
            jax.ShapeDtypeStruct(small.shape, F32),
            jax.ShapeDtypeStruct((4, length // 4, width), BF16),
        ],
        scratch_shapes=[
            vmem((length, width), F32),
            vmem((length, width), BF16),
            vmem((width, width), BF16),
            vmem((length, width), BF16),
            vmem((length, LANES), BF16),
            vmem((short, width), BF16),
            vmem((short, width), BF16),
            vmem((width // LANES, length + 8, LANES), F32),
            vmem((length, width), BF16),
            vmem((width, length), BF16),
            vmem((width, length), BF16),
            vmem((length, width), F32),
            vmem((length, width), BF16),
            vmem((length, width), BF16),
            vmem((length, 3 * width), BF16),
            vmem((length, LANES), BF16),
            vmem((length, LANES), BF16),
            vmem((length, LANES), BF16),
            vmem((length, LANES), F32),
            vmem((length, LANES), F32),
            vmem((width, wide), BF16),
            vmem((width, wide), BF16),
            vmem(out_grad.shape, BF16),
            vmem(up_grad.shape, BF16),
            vmem(down_grad.shape, BF16),
            vmem(small.shape, F32),
            vmem(small.shape, F32),
            vmem((4, length // 4, width), BF16),
        ]
        + scaled(1)
        + scaled(1)
        + scaled(2)
        + [vmem((LINE - 1, rows // SQUARE, cols), BF16) for rows, cols in shapes]
        + [vmem(small.shape, F32)] * 2
        + [vmem((LINE,) + small.shape, F32)]
        + [pltpu.SemaphoreType.DMA((7,))]
        + semaphores(count)
        + semaphores(count)
        + semaphores(count, LINE - 1)
        + semaphores(count, LINE - 1)
        + semaphores(count)
        + semaphores(2 + LINE - 1)
        + semaphores(4)
        + [pltpu.SemaphoreType.DMA((count + 1, 3)), pltpu.SemaphoreType.DMA((16,))]
        + semaphores(1),
        compiler_params=pltpu.CompilerParams(
            collective_id=1, has_side_effects=True, vmem_limit_bytes=VMEM_LIMIT
        ),
        name="last",
    )(
        hidden, gains, proj, key_mark, middle, attended, out_weight, keep, grouped, added,
        active, slant, up_weight, down_weight, query, keyval, keyval,
        pooled_grad, short_result, even, out_grad, up_grad, down_grad, small,
    )
    parts = results[-1]
    results = results[:-1]
    squares = lax.axis_size("dp") // SQUARE
    if squares > 1:
        members = [
            [number * SQUARE + place for number in range(squares)] for place in range(SQUARE)
        ]
        results = lax.psum(results, "dp", axis_index_groups=members)
    return results, parts


def widen_kernel(*refs):
    step = pl.program_id(0)
    half = pl.num_programs(0) // 2
    *sources, parts_ref = refs[: len(refs) // 2]
    *targets, input_ref, results_ref = refs[len(refs) // 2 :]
    for source, target in zip(sources, targets):
        target[...] = source[...].astype(F32)

    @pl.when(step < half)
    def _():
        input_ref[...] = parts_ref[...].astype(F32)

    @pl.when(step >= half)
    def _():
        results_ref[...] = parts_ref[...]


def widen_call(grads, parts):
    steps = parts.shape[0]
    half = steps // 2
    block = lambda value: pl.BlockSpec(
        (value.shape[0] // steps, value.shape[1]), lambda step: (step, 0)
    )
    page = (1,) + parts.shape[1:]
    return pl.pallas_call(
        widen_kernel,
        grid=(steps,),
        in_specs=[block(value) for value in grads]
        + [pl.BlockSpec(page, lambda step: (step, 0, 0))],
        out_specs=[block(value) for value in grads]
        + [
            pl.BlockSpec(page, lambda step: (jnp.minimum(step, half - 1), 0, 0)),
            pl.BlockSpec(page, lambda step: (jnp.maximum(step - half, 0), 0, 0)),
        ],
        out_shape=[jax.ShapeDtypeStruct(value.shape, F32) for value in grads]
        + [
            jax.ShapeDtypeStruct((half,) + parts.shape[1:], F32),
            jax.ShapeDtypeStruct((half,) + parts.shape[1:], BF16),
        ],
        compiler_params=params(),
        name="widen",
    )(*grads, parts)


def body(
    activations,
    cotangent,
    article_ids,
    section_proj,
    out_rows,
    up_rows,
    down_rows,
    norm_gains,
    slopes,
):
    section = lax.axis_index("section")
    core = section % 2
    first_chip = section < 2
    width = activations.shape[3]
    length = article_ids.shape[2]
    short = length // 3
    heads = 2 * slopes.shape[1]
    tile = length // 3

    (
        row, proj, out_weight, up_weight, down_weight, query, keyval, attended, middle, active,
        slant, grouped, long_rows, pooled, short_grad, gains, key_mark, short_query_mark,
        short_key_mark, keep,
    ) = first_call(
        activations, cotangent, article_ids, norm_gains, slopes, section_proj[0], out_rows,
        up_rows, down_rows, heads, tile,
    )
    exchanged = lax.ppermute(long_rows, "section", [(0, 2), (1, 3), (2, 0), (3, 1)])

    def zeros_of(call, *operands):
        return jax.tree.map(
            lambda leaf: jnp.zeros(leaf.shape, leaf.dtype), jax.eval_shape(call, *operands)
        )

    def short_all(pooled, grad):
        return short_call(
            pooled, grad, gains, short_query_mark, short_key_mark, proj, out_weight, up_weight,
            down_weight, heads,
        )

    short_result, pooled_grad, *short_grads = lax.cond(
        first_chip,
        lambda *operands: zeros_of(short_all, *operands),
        short_all,
        pooled,
        short_grad,
    )
    (proj_grad, out_grad, up_grad, down_grad, small), parts = last_call(
        row, gains, proj, key_mark, middle, attended, out_weight, keep, grouped, exchanged,
        active, slant, up_weight, down_weight, query, keyval,
        pooled_grad, short_result, *short_grads, tile=tile,
    )
    proj_grad, out_grad, up_grad, down_grad, input_grad, results = widen_call(
        (proj_grad, out_grad, up_grad, down_grad), parts
    )
    slope_grad = lax.dynamic_slice_in_dim(small[2], core * (heads // 2), heads // 2, 0)
    small = lax.dynamic_slice_in_dim(small, core, 1, 0)
    return (
        results[:, None],
        input_grad[:, None],
        proj_grad[None],
        out_grad,
        up_grad,
        down_grad,
        small,
        slope_grad.reshape(1, heads // 2),
    )


def solution(mesh):
    return jax.shard_map(
        body,
        mesh=mesh,
        in_specs=(
            P(None, "dp", "section", None),
            P(None, "dp", "section", None),
            P(None, "dp", None),
            P("section", None, None),
            P("section", None),
            P("section", None),
            P("section", None),
            P("section", None),
            P("section", None),
        ),
        out_specs=(
            P(None, "dp", "section", None),
            P(None, "dp", "section", None),
            P("section", None, None),
            P("section", None),
            P("section", None),
            P("section", None),
            P("section", None),
            P("section", None),
        ),
        check_vma=False,
    )
```

time: 1940 us -> 221 us (0.11)
  waiting for transfers between devices: 719 us -> 20.2 us
  local copies, waits for them, and re-layouts: 423 us -> 7.87 us
  matrix products: 329 us -> 0 us
  loops' own time: 208 us -> 0.01 us
  Pallas kernels: 0 us -> 191 us
  other arithmetic: 144 us -> 0 us
  starting transfers between devices: 77.8 us -> 4.39 us
    psum x1 -> x0, waiting for transfers between devices: 390 us -> none  [body(): summed = lax.psum((proj_grad,) + tuple(block_grads), 'dp')]
    dot_general x80 -> x0, matrix products: 329 us -> none  [the longest x16 75.6 us: block_scores(): jnp.einsum('bqhd,bkhd->bhqk', queries[:, row_start:row_stop, head_start:h...]
    ppermute x40 -> x1, waiting for transfers between devices: 228 us -> 20.2 us  [body(): lax.ppermute(long_rows, 'section', [(0, 2), (1, 3), (2, 0), (3, 1)])]
    another operation x12 -> x1, loops' own time: 208 us -> 0.01 us  [body(): lax.cond(first_chip, lambda *operands: zeros_of(short_all, *operands), sh...]
    pallas_call x0 -> x3, Pallas kernels: none -> 191 us  [the longest x1 138 us: last_call(): pl.pallas_call(functools.partial(last_kernel, tile=tile), grid=(2 + PARTS...]
    dynamic_update_slice x80 -> x0, local copies, waits for them, and re-layouts: 135 us -> none  [store_one(): lax.dynamic_update_index_in_dim(whole_buf, piece_val.astype(whole_buf.dty...]
    reduce_sum x22 -> x0, other arithmetic: 81.8 us -> none  [the longest x4 47.6 us: attend_back(): jnp.sum(grad_scores.astype(jnp.float32) * distance, axis=(0, 2, 3))]
    another operation x58 -> x7, local copies, waits for them, and re-layouts: 82 us -> 5.91 us
  transfers between devices with their start and end apart: 45 -> 1, of which waited for: 12 -> 1; matrix products, arithmetic and copies ran while one was open for 10% -> 3% of each run, Pallas kernels for 0% -> 0%
where the time goes in v1:
time: 221 us; the launch traced here: 224 us
  Pallas kernels  191 us (86%)
  waiting for transfers between devices  20.2 us (9%)
  local copies, waits for them, and re-layouts  7.87 us (4%)
  starting transfers between devices  4.39 us (2%)
    pallas_call x1, Pallas kernels, last_call(): pl.pallas_call(functools.partial(last_kernel, tile=tile), grid=(2 + PARTS...  138 us
    pallas_call x1, Pallas kernels, first_call(): pl.pallas_call(functools.partial(first_kernel, tile=tile, heads=heads), i...  46.6 us
    ppermute x1, waiting for transfers between devices, body(): lax.ppermute(long_rows, 'section', [(0, 2), (1, 3), (2, 0), (3, 1)])  20.2 us
    pallas_call x1, Pallas kernels, widen_call(): pl.pallas_call(widen_kernel, grid=(steps,), in_specs=[block(value) for va...  6.49 us
    another operation x7, local copies, waits for them, and re-layouts  5.91 us
  transfers between devices with their start and end apart: 1, of which 1 were waited for; matrix products, arithmetic and copies ran while one was open for 3% of the time, Pallas kernels for 0%

profile of v1, /device:TPU:0, one launch (start us, length us, event | category | flops | bytes accessed | tf_op | source)
XLA Modules:
  0.0 224.4 jit_solution(15918865039612648773)
XLA Ops:
  0.6 46.6 %first.1 = (bf16[1152,512]{1,0:T(8,128)(2,1)}, bf16[1024,1536]{1,0:T(8,128)(2,1)S(1)}, bf16[512,512]{1,0:T(8,128)(2,1)}, bf16[512,2048]{1,0:T(8,128)(2,1)}, bf16...) custom-call(bf16[2,1,288,512]{3,2,1,0:T(8,128)(2,1)} %act_ref.1, ...), custom_call_target="tpu_custom_call" | custom-call | tf_op jit(solution)/shard_map/first/pallas_call | solution.py:631
  47.2 4.4 %collective-permute-start = (bf16[1152,512]{1,0:T(8,128)(2,1)}, bf16[1152,512]{1,0:T(8,128)(2,1)}, u32[]{:S(2)}, u32[]{:S(2)}) collective-permute-start(bf16[1152,512]{1,0:T(8,128)(2,1)} %get-tuple-element.83), channel_id=1, source_target_pairs={{0,16},{8,24},{16,0},{24,8},{1,17},{9,25},{17,1},{25,9},{2,18},{10... | collective-permute-start | bytes 3538952 | tf_op jit(solution)/shard_map/ppermute | solution.py:1764
  51.6 5.9 %conditional.1 = ((bf16[384,512]{1,0:T(8,128)(2,1)S(1)}, bf16[384,512]{1,0:T(8,128)(2,1)}, bf16[512,1536]{1,0:T(8,128)(2,1)}, bf16[512,512]{1,0:T(8,128)(2,1)}, ...) conditional(s32[]{:T(128)} %convert_element_type.3, ...), branch_computations={%region_0.1_spmd, %region_1.2_spmd} | conditional | bytes 7094352 | solution.py:1777
  51.6 0.8 broadcast.13.clone
  52.4 1.2 broadcast.14
  53.6 0.8 broadcast.15
  54.5 1.6 broadcast.16
  56.0 1.5 broadcast.17
  57.5 20.2 %collective-permute-done.added_ref = bf16[1152,512]{1,0:T(8,128)(2,1)} collective-permute-done((bf16[1152,512]{1,0:T(8,128)(2,1)}, bf16[1152,512]{1,0:T(8,128)(2,1)}, u32[]{:S(2)}, u32[]{:S(2)}) %collective-permute-start) | collective-permute-done | bytes 1179680 | tf_op jit(solution)/shard_map/ppermute | solution.py:1764
  77.7 138.1 %last.1 = (bf16[512,1536]{1,0:T(8,128)(2,1)}, bf16[256,512]{1,0:T(8,128)(2,1)}, bf16[256,2048]{1,0:T(8,128)(2,1)}, bf16[1024,512]{1,0:T(8,128)(2,1)}, f32[8,512]{1,0:T(8,128)}, /*index=5*/bf16[4,288,512]{2,1,0:T(8,128)(2,1)}) custom-call(bf16[1152,512]{1,0:T(8,128)(2,1)} %get-tuple-element.74.hidden_src, f32[16,512]{1,0:T(8,128)} %get-tuple-element.75.gain_ref, ...), custom_call_target="tpu_custom_call" | custom-call | tf_op jit(solution)/shard_map/last/pallas_call | solution.py:1607
  215.8 1.4 fusion
  217.2 0.6 constant_dynamic-slice_fusion
  217.7 6.5 %widen.1 = (f32[512,1536]{1,0:T(8,128)}, f32[256,512]{1,0:T(8,128)}, f32[256,2048]{1,0:T(8,128)}, f32[1024,512]{1,0:T(8,128)}, f32[2,288,512]{2,1,0:T(8,128)}, /*index=5*/bf16[2,288,512]{2,1,0:T(8,128)(2,1)}) custom-call(bf16[512,1536]{1,0:T(8,128)(2,1)} %get-tuple-element.101.refs_0_, bf16[256,512]{1,0:T(8,128)(2,1)} %get-tuple-element.102.refs_1_, ...), custom_call_target="tpu_custom_call" | custom-call | tf_op jit(solution)/shard_map/widen/pallas_call | solution.py:1716
  (2 shorter events, 0.0 us)
Async XLA Ops:
  47.2 30.5 %collective-permute-start = (bf16[1152,512]{1,0:T(8,128)(2,1)}, bf16[1152,512]{1,0:T(8,128)(2,1)}, u32[]{:S(2)}, u32[]{:S(2)}) collective-permute-start(bf16[1152,512]{1,0:T(8,128)(2,1)} %get-tuple-element.83), channel_id=1, source_target_pairs={{0,16},{8,24},{16,0},{24,8},{1,17},{9,25},{17,1},{25,9},{2,18},{10... | collective-permute-start | bytes 3538952 | tf_op jit(solution)/shard_map/ppermute | solution.py:1764
